TPU v7x, 128 devices: a whole 4x4x4 slice. The times are simulated.
128 devices in a mesh: frame: 8 (over z, y_lo), height: 8 (over y_hi, x), head: 2 (over core).
Axes of the slice: x: 4, y: 4 (y_hi: 2, y_lo: 2; y = y_hi * 2 + y_lo), z: 4, core: 2. Of those that a mesh axis runs over, the one named last changes fastest.
Arguments:
- queries: bfloat16 [16, 64, 48, 2560], P(('frame', 'head'), 'height'), may hold values from -112 to 112
- keys: bfloat16 [16, 64, 48, 2560], P(('frame', 'head'), 'height'), may hold values from -4 to 4
- values: bfloat16 [16, 64, 48, 2560], P(('frame', 'head'), 'height'), may hold values from -6 to 6
- out_weight: bfloat16 [2560, 5120], P('head'), may hold values from -0.25 to 0.25
- window_radii: int32 [20, 3], replicated, may hold values from 0 to 1
- frame_valid: int32 [16], replicated, may hold values from 0 to 1, as said below
Outputs:
- projected: bfloat16 [16, 64, 48, 5120], P(('frame', 'head'), 'height')
Inputs may be any that keep to these rules, and one draw needn't show every extreme that they name: `frame_valid`: padding frames form a run of 0 to 2 frames at the start and a run of 1 to 2 frames at the end.
All inputs are finite; a program needn't handle non-finite values.
Results may differ from a plain program's by a relative error of at most 0.0057.
Values may be sent and summed in bfloat16 or wider, within the bound.
No kernel may reach another device: no remote copies, remote signals or barrier semaphores. Data moves between devices by JAX's collectives and lax.ppermute only.
A program may use at most 192 MiB of HBM per device.

v0:
```python
import functools
import math

import jax
import jax.numpy as jnp
import numpy as np
from jax import lax
from jax.experimental import pallas as pl
from jax.experimental.pallas import tpu as pltpu
from jax.sharding import PartitionSpec as P

HEAD_DIM = 128
ROW_TILE = 2
COL_TILE = 16
NEG_FILL = -1e30
GRID_AXES = ("frame", "head")
VMEM_BYTES = 62 * 1024 * 1024
SCALE = HEAD_DIM ** -0.5 * math.log2(math.e)


def plan_heads(window_radii, frame_valid, levels):
    heads = window_radii.shape[0]
    frames = frame_valid.shape[0]

    def kernel(radii_ref, valid_ref, meta_ref, slot_ref, flag_ref, level_ref):
        both, side, edge = (jnp.int32(0) for _ in range(3))
        for head in range(heads):
            rad_f, rad_r = radii_ref[head, 0], radii_ref[head, 1]
            both += rad_f * rad_r
            side += rad_f * (1 - rad_r)
            edge += (1 - rad_f) * rad_r
        starts = [both + side + edge, both + side, both, 0]
        for head in range(heads):
            rad_f, rad_r = radii_ref[head, 0], radii_ref[head, 1]
            kind = 2 * rad_f + rad_r
            place = sum(jnp.where(kind == i, starts[i], 0) for i in range(4))
            slot = place + jnp.where(kind == 2, edge, 0) - jnp.where(kind == 1, side, 0)
            starts = [starts[i] + (kind == i).astype(jnp.int32) for i in range(4)]
            meta_ref[0, place] = head
            meta_ref[1, place] = rad_f
            meta_ref[2, place] = rad_r
            meta_ref[3, place] = radii_ref[head, 2]
            meta_ref[4, place] = slot
            meta_ref[5, place] = head // (heads // 2)
            meta_ref[6, place] = head % (heads // 2)
            slot_ref[slot] = head
        part = lax.axis_index("head")
        frame = 2 * lax.axis_index("frame") + part
        height = lax.axis_index("height")
        inner, outer = frame + 1 - 2 * part, frame - 1 + 2 * part
        outer_ok = (outer >= 0) & (outer < frames) & (valid_ref[jnp.clip(outer, 0, frames - 1)] == 1)
        flag_ref[0] = (valid_ref[inner] == 1).astype(jnp.int32)
        flag_ref[1] = outer_ok.astype(jnp.int32)
        flag_ref[2] = (height > 0).astype(jnp.int32)
        flag_ref[3] = (height < lax.axis_size("height") - 1).astype(jnp.int32)
        flag_ref[4] = part
        level = jnp.int32(0)
        for i, (most_side, most_both, most_edge) in enumerate(levels):
            fits = (both + side <= most_side) & (both <= most_both) & (both + edge <= most_edge)
            level = jnp.where(fits, i, level)
        level_ref[0] = level

    smem = pl.BlockSpec(memory_space=pltpu.SMEM)
    shapes = [(8, heads), (heads,), (8,), (1,)]
    return pl.pallas_call(
        kernel,
        out_shape=[jax.ShapeDtypeStruct(shape, jnp.int32) for shape in shapes],
        in_specs=[smem, smem],
        out_specs=[smem] * len(shapes),
    )(window_radii, frame_valid)


def pack_heads(order, sources, groups, tile, tiles, slots=None, edge_groups=()):
    tokens, width = sources[0].shape
    scalars = [order] if slots is None else [order, slots]
    edge_shapes = [(count, len(sources), tile, HEAD_DIM) for _, count in edge_groups]

    def kernel(*refs):
        order_ref, refs = refs[0], refs[len(scalars) - 1 :]
        slot_ref, refs = refs[0], refs[1:]
        ins, outs = refs[: len(sources)], refs[len(sources) :]

        def gather(from_ref, first, count, which, out):
            def copy(at, carry):
                columns = pl.ds(pl.multiple_of(from_ref[first + at] * HEAD_DIM, HEAD_DIM), HEAD_DIM)
                for index, source in enumerate(which):
                    out[at, index] = ins[source][:, columns]
                return carry

            lax.fori_loop(0, count, copy, 0, unroll=2)

        for (first, count, which), out in zip(groups, outs):
            gather(order_ref, first, count, which, out)
        if slots is not None:
            for i, at in enumerate((0, tiles - 1)):

                @pl.when(pl.program_id(0) == at)
                def _():
                    for j, (first, count) in enumerate(edge_groups):
                        gather(slot_ref, first, count, range(len(sources)), outs[len(groups) + 2 * j + i])

    in_spec = pl.BlockSpec((tile, width), lambda step, *refs: (step, 0))
    out_specs = [
        pl.BlockSpec((count, len(which), tile, HEAD_DIM), lambda step, *refs: (0, 0, step, 0))
        for _, count, which in groups
    ]
    shapes = [(count, len(which), tokens, HEAD_DIM) for _, count, which in groups]
    if slots is not None:
        for shape in edge_shapes:
            out_specs += [pl.BlockSpec(shape, lambda step, *refs: (0, 0, 0, 0))] * 2
            shapes += [shape] * 2
    return pl.pallas_call(
        kernel,
        out_shape=[jax.ShapeDtypeStruct(shape, sources[0].dtype) for shape in shapes],
        grid_spec=pltpu.PrefetchScalarGridSpec(
            num_scalar_prefetch=len(scalars),
            grid=(tiles,),
            in_specs=[in_spec] * len(sources),
            out_specs=out_specs,
        ),
        compiler_params=pltpu.CompilerParams(vmem_limit_bytes=VMEM_BYTES),
    )(*scalars, *sources)


def attend(query, keys, values, col_mask, biases, flip):
    scores = lax.dot_general(
        keys, query, (((1,), (1,)), ((), ())), preferred_element_type=jnp.float32
    )
    mask = jnp.concatenate([col_mask if x is None else col_mask + x for x in biases], axis=0)
    scores = scores * SCALE + mask
    expo = jnp.exp2(scores - jnp.max(scores, axis=0, keepdims=True))
    probs = (expo * (1.0 / jnp.sum(expo, axis=0, keepdims=True))).astype(jnp.bfloat16)
    left, right = (values, probs) if flip else (probs, values)
    out = lax.dot_general(left, right, (((0,), (0,)), ((), ())), preferred_element_type=jnp.float32)
    return (out.T if flip else out).astype(jnp.bfloat16)


def chunk(meta, flags, col_masks, first, own, given, weights, block, tile, tiles, unroll=2):
    tokens = tile * tiles
    count = own["query"].shape[0]
    sides, corners, edges = own.get("sides", ()), own.get("corners", ()), own["edges"]
    places = [(start + i, g, i) for g, (start, x) in enumerate(given) for i in range(x.shape[0])]
    depth = weights[0].shape[0] if weights else 0
    width = weights[0].shape[1] if weights else 0
    blocks = width // block
    across = 1 + len(sides)

    def kernel(meta_ref, flag_ref, mask_ref, *refs):
        refs = list(refs)

        def take(items):
            return [refs.pop(0) for _ in items]

        query_ref, pair_ref = take(range(2))
        side_refs, corner_refs = take(sides), take(corners)
        edge_refs = take(edges)
        given_refs, weight_refs = take(given), take(weights)
        out_ref = refs.pop(0)
        query_buf, pair_buf, edge_buf, key_buf, value_buf, attended, own_sem, edge_sem = take(range(8))
        side_buf, corner_buf = take(sides[:1]), take(corners[:1])
        if weights:
            given_sem, weight_buf, weight_sem, out_buf, out_sem = take(range(5))

        def own_copies(at):
            pairs = [(query_ref.at[at], query_buf.at[at]), (pair_ref.at[at], pair_buf.at[at])]
            pairs += [(x.at[at], side_buf[0].at[at, i]) for i, x in enumerate(side_refs)]
            pairs += [(x.at[at], corner_buf[0].at[at, i]) for i, x in enumerate(corner_refs)]
            return [pltpu.make_async_copy(x, y, own_sem.at[at, i]) for i, (x, y) in enumerate(pairs)]

        def edge_copies(at, slot):
            return [
                pltpu.make_async_copy(x.at[slot], edge_buf.at[at, i], edge_sem.at[at, i])
                for i, x in enumerate(edge_refs)
            ]

        def begin_own(at, carry):
            for copy in own_copies(at):
                copy.start()
            slot = meta_ref[4, first + at]

            for copy in edge_copies(at, jnp.minimum(slot, edges[0].shape[0] - 1)):
                copy.start()

            return carry

        def head_columns(place):
            half = jnp.where(meta_ref[5, place] == flag_ref[4], 0, depth)
            return pl.ds(pl.multiple_of(half + meta_ref[6, place] * HEAD_DIM, HEAD_DIM), HEAD_DIM)

        def given_copy(index):
            place, g, i = places[index]
            return pltpu.make_async_copy(
                given_refs[g].at[i], attended.at[:, head_columns(place)], given_sem.at[index]
            )

        def columns(at):
            return pl.ds(pl.multiple_of(at * block, block), block)

        def weight_copies(at):
            return [
                pltpu.make_async_copy(x.at[:, columns(at)], weight_buf.at[i, :, columns(at)], weight_sem.at[i, at])
                for i, x in enumerate(weight_refs)
            ]

        def out_copy(at):
            return pltpu.make_async_copy(out_buf.at[:, columns(at)], out_ref.at[:, columns(at)], out_sem.at[at])

        def begin_share(at, carry):
            for copy in weight_copies(at):
                copy.start()
            return carry

        def tile_rows(at, size=1):
            return pl.ds(pl.multiple_of(at * tile, tile), size * tile)

        def off(ok):
            return jnp.where(ok, 0.0, NEG_FILL)

        def lay(row, source_k, source_v):
            key_buf[tile_rows(row), :] = source_k
            value_buf[tile_rows(row), :] = source_v

        def head_step(head, carry):
            place = first + head
            rad_f, rad_r, rad_c = meta_ref[1, place], meta_ref[2, place], meta_ref[3, place]
            for copy in own_copies(head) + edge_copies(head, 0):
                copy.wait()
            col_mask = mask_ref[rad_c]
            side_bias = [None] + [off((rad_f > 0) & (flag_ref[i] != 0)) for i in range(across - 1)]
            bodies = [pair_buf.at[head]] + [side_buf[0].at[head, i] for i in range(across - 1)]

            def band_bias(at):
                low = off((rad_r > 0) & ((at > 0) | (flag_ref[2] != 0)))
                high = off((rad_r > 0) & ((at < tiles - 1) | (flag_ref[3] != 0)))
                return low, None, high

            def run(at, start, biases, flip):
                rows, held = tile_rows(at), tile_rows(start, len(biases))
                found = attend(
                    query_buf[head, 0, rows, :], key_buf[held, :], value_buf[held, :], col_mask, biases, flip
                )
                if weights:
                    attended[rows, head_columns(place)] = found
                else:
                    attended[head, rows, :] = found

            def fill(band):
                def step(at, carry):
                    rows = tile_rows(at)
                    for which, body in enumerate(bodies):
                        lay(across * (at + band) + which, body[0, rows, :], body[1, rows, :])
                    return carry

                lax.fori_loop(0, tiles, step, 0, unroll=2)

            def with_rows():
                ends = [(edge_buf.at[head, 2 * i], edge_buf.at[head, 2 * i + 1]) for i in range(len(edges) // 2)]
                if corners:
                    ends.append((corner_buf[0].at[head, 0], corner_buf[0].at[head, 1]))
                for which, (low, high) in enumerate(ends):
                    lay(which, low[0], low[1])
                    lay(across * (tiles + 1) + which, high[0], high[1])
                fill(1)

                def each(at, carry):
                    biases = []
                    for x in band_bias(at):
                        for y in side_bias:
                            biases.append(x if y is None else y if x is None else jnp.minimum(x, y))
                    run(at, across * at, biases, across > 1)
                    return carry

                lax.fori_loop(0, tiles, each, 0, unroll=tiles if across == 1 else unroll)

            if sides:
                pl.when(rad_r > 0)(with_rows)

                @pl.when(rad_r == 0)
                def _():
                    fill(0)

                    def each(at, carry):
                        run(at, across * at, side_bias, False)
                        return carry

                    lax.fori_loop(0, tiles, each, 0, unroll=tiles)

            else:
                with_rows()
            return carry

        def share(at, carry):
            for copy in weight_copies(at):
                copy.wait()
            total = sum(
                jnp.dot(
                    attended[:, i * depth : (i + 1) * depth], weight_buf[i, :, columns(at)],
                    preferred_element_type=jnp.float32,
                )
                for i in range(2)
            )
            out_buf[:, columns(at)] = total.astype(out_buf.dtype)
            out_copy(at).start()
            return carry

        def end_share(at, carry):
            out_copy(at).wait()
            return carry

        lax.fori_loop(0, count, begin_own, 0)
        if weights:
            for index in range(len(places)):
                given_copy(index).start()
            lax.fori_loop(0, blocks, begin_share, 0)
        lax.fori_loop(0, count, head_step, 0)
        if weights:
            for index in range(len(places)):
                given_copy(index).wait()
        if weights:
            lax.fori_loop(0, blocks, share, 0)
            lax.fori_loop(0, blocks, end_share, 0)
        else:
            done = pltpu.make_async_copy(attended, out_ref, own_sem.at[0, 0])
            done.start()
            done.wait()

    anywhere, smem = pl.BlockSpec(memory_space=pl.ANY), pl.BlockSpec(memory_space=pltpu.SMEM)
    operands, scratch = [], []
    bf16 = jnp.bfloat16
    operands += [own["query"], own["pair"], *sides, *corners, *edges]
    kinds = 2 + len(sides) + len(corners)
    scratch += [
            pltpu.VMEM(own["query"].shape, bf16),
            pltpu.VMEM(own["pair"].shape, bf16),
            pltpu.VMEM((count, len(edges), 2, tile, HEAD_DIM), bf16),
            pltpu.VMEM((across * (tiles + 2) * tile, HEAD_DIM), bf16),
            pltpu.VMEM((across * (tiles + 2) * tile, HEAD_DIM), bf16),
            pltpu.VMEM((tokens, 2 * depth) if weights else (count, tokens, HEAD_DIM), bf16),
            pltpu.SemaphoreType.DMA((count, kinds)),
            pltpu.SemaphoreType.DMA((count, len(edges))),
        ]
    if sides:
        scratch.append(pltpu.VMEM((count, 2, 2, tokens, HEAD_DIM), bf16))
    if corners:
        scratch.append(pltpu.VMEM((count, 2, 2, tile, HEAD_DIM), bf16))
    operands += [x for _, x in given]
    out_type = bf16
    if weights:
        operands += list(weights)
        scratch += [
            pltpu.SemaphoreType.DMA((len(places),)),
            pltpu.VMEM((2, depth, width), bf16),
            pltpu.SemaphoreType.DMA((2, blocks)),
            pltpu.VMEM((tokens, width), out_type),
            pltpu.SemaphoreType.DMA((blocks,)),
        ]
    shape = (tokens, width) if weights else (count, tokens, HEAD_DIM)
    return pl.pallas_call(
        kernel,
        out_shape=jax.ShapeDtypeStruct(shape, out_type),
        in_specs=[smem, smem, pl.BlockSpec(memory_space=pltpu.VMEM)] + [anywhere] * len(operands),
        out_specs=anywhere,
        scratch_shapes=scratch,
        compiler_params=pltpu.CompilerParams(vmem_limit_bytes=VMEM_BYTES),
    )(meta, flags, col_masks, *operands)


def on_device(queries, keys, values, out_weight, window_radii, frame_valid):
    _, rows_dev, col_total, width = queries.shape
    heads = width // HEAD_DIM
    tile = ROW_TILE * col_total
    tiles = rows_dev // ROW_TILE
    tokens = tile * tiles
    frame_pairs, height_total = lax.axis_size("frame"), lax.axis_size("height")
    q, k, v = (x.reshape(tokens, width) for x in (queries, keys, values))
    outer_pairs = [(2 * i + 1, 2 * i + 2) for i in range(frame_pairs - 1)]
    outer_pairs += [(target, source) for source, target in outer_pairs]
    swap = [(0, 1), (1, 0)]
    down = [(i, i + 1) for i in range(height_total - 1)]
    up = [(i + 1, i) for i in range(height_total - 1)]
    levels = [(heads, heads, heads), (16, 10, 16), (13, 8, 14), (10, 6, 12)]

    meta, slots, flags, level = plan_heads(window_radii, frame_valid, levels)
    order = meta[0]

    col = np.arange(tile) % col_total // COL_TILE
    gap = np.abs(col[:, None] - col[None, :])
    col_masks = jnp.asarray(np.stack([np.where(gap <= x, 0.0, NEG_FILL) for x in range(2)]).astype(np.float32))

    def trade_edges(low, high):
        return lax.ppermute(high, "height", down), lax.ppermute(low, "height", up)

    def to_sibling(pair):
        return tuple(lax.ppermute(x, "head", swap) for x in pair)

    def trade_corners(beyond):
        return (
            lax.ppermute(beyond[:, :, tokens - tile :], "height", down),
            lax.ppermute(beyond[:, :, :tile], "height", up),
        )

    def finish(side_count, both_count, edge_count):
        def call(q, k, v, out_weight):
            size = both_count if both_count < side_count else side_count // 2
            parts = [(0, size), (size, side_count - size)]
            rest = heads - side_count
            *packed, low, high = pack_heads(
                order, (k, v), [(*x, (0, 1)) for x in parts], tile, tiles, slots, [(0, edge_count)]
            )
            beyond = [lax.ppermute(x, GRID_AXES, outer_pairs) for x in packed]
            beside = [lax.ppermute(x, "head", swap) for x in packed]
            weights = (out_weight, lax.ppermute(out_weight, "head", swap))
            edges = trade_edges(low, high)
            groups = [(*x, (0,)) for x in parts]
            groups += [(side_count, rest, (0,)), (side_count, rest, (1, 2))] if rest else []
            ordered = pack_heads(order, (q, k, v), groups, tile, tiles)
            edges, ordered = lax.optimization_barrier((edges, ordered))
            edges += to_sibling(edges)
            edges, ordered = lax.optimization_barrier((edges, ordered))
            common = (meta, flags, col_masks)
            shared = []
            near = beyond[0]
            if rest:
                own = {"query": ordered[2], "pair": ordered[3], "edges": edges[:2]}
                lone = chunk(*common, side_count, own, [], (), 1024, tile, tiles)
                near, lone = lax.optimization_barrier((near, lone))
                shared.append((side_count, lone))
            corners = trade_corners(near)
            own = {"query": ordered[0], "pair": packed[0], "sides": (beside[0], near), "edges": edges, "corners": corners}
            first = chunk(*common, 0, own, [], (), 1024, tile, tiles, 4)
            far, first = lax.optimization_barrier((beyond[1], first))
            shared.append((0, first))
            if both_count > size:
                corners = trade_corners(far)
            own = {"query": ordered[1], "pair": packed[1], "sides": (beside[1], far), "edges": edges, "corners": corners}
            return chunk(*common, size, own, shared, weights, 1024, tile, tiles)

        return call

    projected = lax.switch(level[0], [finish(*x) for x in levels], q, k, v, out_weight)
    return projected.reshape(1, rows_dev, col_total, out_weight.shape[1])


def solution(mesh):
    return jax.shard_map(
        on_device,
        mesh=mesh,
        in_specs=(
            P(("frame", "head"), "height", None, None),
            P(("frame", "head"), "height", None, None),
            P(("frame", "head"), "height", None, None),
            P("head", None),
            P(),
            P(),
        ),
        out_specs=P(("frame", "head"), "height", None, None),
        check_vma=False,
    )
```

profile of v0, /device:TPU:95, one launch (start us, length us, event | category | flops | bytes accessed | tf_op | source)
XLA Modules:
  0.0 127.3 jit_solution(11581067052850075922)
XLA Ops:
  0.0 1.4 %copy.12.radii_ref = s32[20,3]{1,0:T(8,128)} copy(s32[20,3]{0,1:T(4,128)} %param.15) | data formatting | bytes 480 | tf_op args[4]
  1.4 1.9 %shard_map.77 = (s32[8,20]{1,0:T(8,128)S(1)}, s32[20]{0:T(128)S(1)}, s32[8]{0:T(128)S(1)}, s32[1]{0:T(128)}) custom-call(s32[20,3]{1,0:T(8,128)} %copy.12.radii_ref, s32[16]{0:T(128)} %valid_ref.1), custom_call_target="tpu_custom_call" | custom-call | tf_op jit(solution)/shard_map/pallas_call | solution.py:65
  3.9 123.1 %conditional.1 = (bf16[1,8,48,5120]{3,2,1,0:T(8,128)(2,1)}) conditional(s32[]{:T(128)} %bitcast.4, (s32[20]{0:T(128)S(1)}, s32[20]{0:T(128)S(1)}, bf16[384,2560]{1,0:T(8,128)(2,1)}, bf16[384,2560]{1,0:T(8,128)(2,1)}, bf16[384,2560]{1,0:T(8,128)(2,1)}, /*index=5*/s32[8,20]{1,0:T(8,128)S(1)}, s32[8]{0:T(128)S(1)}, ...), branch_computations={%region_0.0_spmd, %region_1.0_spmd, %region_2.0_spmd, %region_3.0_... | conditional | bytes 129401528 | solution.py:440
  4.2 0.8 collective-permute-start.34
  4.9 0.0 copy-start.2
  4.9 5.8 %branch_2_fun.5 = (bf16[8,2,384,128]{3,2,1,0:T(8,128)(2,1)}, bf16[5,2,384,128]{3,2,1,0:T(8,128)(2,1)}, bf16[14,2,96,128]{3,2,1,0:T(8,128)(2,1)}, bf16[14,2,96,128]{3,2,1,0:T(8,128)(2,1)}) custom-call(s32[20]{0:T(128)S(1)} %get-tuple-element.148.refs_0_, s32[20]{0:T(128)S(1)} %get-tuple-element.149.refs_1_, bf16[384,2560]{1,0:T(8,128)(2,1)} %get-tuple-element.150.refs_2_, ...), custom_call_target="tpu_custom_call" | custom-call | tf_op jit(solution)/shard_map/cond/branch_2_fun/pallas_call | solution.py:112
  10.8 1.3 %collective-permute-start.24 = (bf16[14,2,96,128]{3,2,1,0:T(8,128)(2,1)}, bf16[14,2,96,128]{3,2,1,0:T(8,128)(2,1)}, u32[]{:S(2)}, u32[]{:S(2)}) collective-permute-start(bf16[14,2,96,128]{3,2,1,0:T(8,128)(2,1)} %get-tuple-element.152), channel_id=1, source_target_pairs={{0,2},{2,4},{4,6},{6,8},{8,10},{10,12},{12,14},{1,3},{3,5},{5,7},{... | collective-permute-start | bytes 2064392 | tf_op jit(solution)/shard_map/cond/branch_2_fun/ppermute | solution.py:391
  12.1 4.9 %collective-permute-start.25 = (bf16[14,2,96,128]{3,2,1,0:T(8,128)(2,1)}, bf16[14,2,96,128]{3,2,1,0:T(8,128)(2,1)}, u32[]{:S(2)}, u32[]{:S(2)}) collective-permute-start(bf16[14,2,96,128]{3,2,1,0:T(8,128)(2,1)} %get-tuple-element.153), channel_id=1, source_target_pairs={{2,0},{4,2},{6,4},{8,6},{10,8},{12,10},{14,12},{3,1},{5,3},{7,5},{... | collective-permute-start | bytes 2064392 | tf_op jit(solution)/shard_map/cond/branch_2_fun/ppermute | solution.py:391
  16.9 3.9 %collective-permute-start.31 = (bf16[8,2,384,128]{3,2,1,0:T(8,128)(2,1)}, bf16[8,2,384,128]{3,2,1,0:T(8,128)(2,1)}, u32[]{:S(2)}, u32[]{:S(2)}) collective-permute-start(bf16[8,2,384,128]{3,2,1,0:T(8,128)(2,1)} %get-tuple-element.168.refs_1_), channel_id=1, source_target_pairs={{1,16},{17,32},{33,48},{49,64},{65,80},{81,96},{97,112},{16,1},{32... | collective-permute-start | bytes 4718600 | tf_op jit(solution)/shard_map/cond/branch_2_fun/ppermute | solution.py:410
  20.8 0.1 collective-permute-start.30
  20.9 0.0 copy-done.2
  20.9 5.4 %branch_2_fun.6 = (bf16[8,1,384,128]{3,2,1,0:T(8,128)(2,1)}, bf16[5,1,384,128]{3,2,1,0:T(8,128)(2,1)}, bf16[7,1,384,128]{3,2,1,0:T(8,128)(2,1)}, bf16[7,2,384,128]{3,2,1,0:T(8,128)(2,1)}) custom-call(s32[20]{0:T(128)S(1)} %get-tuple-element.148.refs_0_, bf16[384,2560]{1,0:T(8,128)(2,1)} %get-tuple-element.154.refs_1_, bf16[384,2560]{1,0:T(8,128)(2,1)S(1)} %copy-done.2, ...), custom_call_target="tpu_custom_call" | custom-call | tf_op jit(solution)/shard_map/cond/branch_2_fun/pallas_call | solution.py:112
  26.3 3.7 %collective-permute-done.24.refs_2_.refs_6_ = bf16[14,2,96,128]{3,2,1,0:T(8,128)(2,1)} collective-permute-done((bf16[14,2,96,128]{3,2,1,0:T(8,128)(2,1)}, bf16[14,2,96,128]{3,2,1,0:T(8,128)(2,1)}, u32[]{:S(2)}, u32[]{:S(2)}) %collective-permute-start.24) | collective-permute-done | bytes 688160 | tf_op jit(solution)/shard_map/cond/branch_2_fun/ppermute | solution.py:391
  30.0 0.9 collective-permute-done.25.refs_3_.refs_7_
  30.9 1.1 collective-permute-start.26
  32.0 0.0 collective-permute-start.27
  32.0 2.0 %collective-permute-done.26.refs_8_ = bf16[14,2,96,128]{3,2,1,0:T(8,128)(2,1)S(1)} collective-permute-done((bf16[14,2,96,128]{3,2,1,0:T(8,128)(2,1)}, bf16[14,2,96,128]{3,2,1,0:T(8,128)(2,1)S(1)}, u32[]{:S(2)}, u32[]{:S(2)}) %collective-permute-start.26) | collective-permute-done | bytes 688160 | tf_op jit(solution)/shard_map/cond/branch_2_fun/ppermute | solution.py:394
  34.0 0.0 copy-start.11
  34.0 3.7 %collective-permute-start.29 = (bf16[5,2,384,128]{3,2,1,0:T(8,128)(2,1)}, bf16[5,2,384,128]{3,2,1,0:T(8,128)(2,1)}, u32[]{:S(2)}, u32[]{:S(2)}) collective-permute-start(bf16[5,2,384,128]{3,2,1,0:T(8,128)(2,1)} %get-tuple-element.166.refs_1_), channel_id=1, source_target_pairs={{1,16},{17,32},{33,48},{49,64},{65,80},{81,96},{97,112},{16,1},{32... | collective-permute-start | bytes 2949128 | tf_op jit(solution)/shard_map/cond/branch_2_fun/ppermute | solution.py:410
  37.7 0.0 collective-permute-done.27.refs_9_
  37.7 0.0 copy-start.12
  37.7 0.1 collective-permute-start.28
  37.8 0.0 copy-start.6
  37.8 7.7 %branch_2_fun.7.refs_10_ = bf16[7,384,128]{2,1,0:T(8,128)(2,1)} custom-call(s32[8,20]{1,0:T(8,128)S(1)} %get-tuple-element.145.meta_ref, s32[8]{0:T(128)S(1)} %get-tuple-element.146.flag_ref, f32[2,96,96]{2,1,0:T(8,128)} %get-tuple-element.147.mask_ref, bf16[7,1,384,128]{3,2,1,0:T(8,128)(2,1)} %get-tuple-element.169.refs_0_, ...), custom_call_target="tpu_custom_call" | custom-call | tf_op jit(solution)/shard_map/cond/branch_2_fun/pallas_call | solution.py:358
  45.6 0.0 copy-done.11
  45.6 0.0 copy-done.12
  45.6 33.7 %collective-permute-done.31.refs_3_ = bf16[8,2,384,128]{3,2,1,0:T(8,128)(2,1)} collective-permute-done((bf16[8,2,384,128]{3,2,1,0:T(8,128)(2,1)}, bf16[8,2,384,128]{3,2,1,0:T(8,128)(2,1)}, u32[]{:S(2)}, u32[]{:S(2)}) %collective-permute-start.31) | collective-permute-done | bytes 1572896 | tf_op jit(solution)/shard_map/cond/branch_2_fun/ppermute | solution.py:410
  79.2 1.2 fusion.3
  80.4 1.3 %collective-permute-start.33 = (bf16[8,2,96,128]{3,2,1,0:T(8,128)(2,1)S(1)}, bf16[8,2,96,128]{3,2,1,0:T(8,128)(2,1)S(1)}, u32[]{:S(2)}, u32[]{:S(2)}) collective-permute-start(bf16[8,2,96,128]{3,2,1,0:T(8,128)(2,1)S(1)} %get-tuple-element.230), channel_id=1, source_target_pairs={{2,0},{4,2},{6,4},{8,6},{10,8},{12,10},{14,12},{3,1},{5,3},{7,5},{... | collective-permute-start | bytes 1179656 | tf_op jit(solution)/shard_map/cond/branch_2_fun/ppermute | solution.py:399
  81.7 0.0 collective-permute-done.30.refs_2_
  81.8 1.3 %collective-permute-start.32 = (bf16[8,2,96,128]{3,2,1,0:T(8,128)(2,1)S(1)}, bf16[8,2,96,128]{3,2,1,0:T(8,128)(2,1)S(1)}, u32[]{:S(2)}, u32[]{:S(2)}) collective-permute-start(bf16[8,2,96,128]{3,2,1,0:T(8,128)(2,1)S(1)} %get-tuple-element.231), channel_id=1, source_target_pairs={{0,2},{2,4},{4,6},{6,8},{8,10},{10,12},{12,14},{1,3},{3,5},{5,7},{... | collective-permute-start | bytes 1179656 | tf_op jit(solution)/shard_map/cond/branch_2_fun/ppermute | solution.py:398
  83.1 7.5 %collective-permute-done.33.refs_5_ = bf16[8,2,96,128]{3,2,1,0:T(8,128)(2,1)S(1)} collective-permute-done((bf16[8,2,96,128]{3,2,1,0:T(8,128)(2,1)S(1)}, bf16[8,2,96,128]{3,2,1,0:T(8,128)(2,1)S(1)}, u32[]{:S(2)}, u32[]{:S(2)}) %collective-permute-start.33) | collective-permute-done | bytes 393248 | tf_op jit(solution)/shard_map/cond/branch_2_fun/ppermute | solution.py:399
  90.5 0.0 copy-start.17
  90.6 4.2 %collective-permute-done.32.refs_4_ = bf16[8,2,96,128]{3,2,1,0:T(8,128)(2,1)S(1)} collective-permute-done((bf16[8,2,96,128]{3,2,1,0:T(8,128)(2,1)S(1)}, bf16[8,2,96,128]{3,2,1,0:T(8,128)(2,1)S(1)}, u32[]{:S(2)}, u32[]{:S(2)}) %collective-permute-start.32) | collective-permute-done | bytes 393248 | tf_op jit(solution)/shard_map/cond/branch_2_fun/ppermute | solution.py:398
  94.8 0.0 copy-done.17
  94.8 0.0 copy-start.18
  94.8 0.7 copy-done.18
  95.5 0.0 copy-done.6
  95.5 13.4 %branch_2_fun.8.refs_11_ = bf16[8,384,128]{2,1,0:T(8,128)(2,1)} custom-call(s32[8,20]{1,0:T(8,128)S(1)} %get-tuple-element.145.meta_ref, s32[8]{0:T(128)S(1)} %get-tuple-element.146.flag_ref, f32[2,96,96]{2,1,0:T(8,128)S(1)} %copy-done.6, bf16[8,1,384,128]{3,2,1,0:T(8,128)(2,1)} %get-tuple-element.167.refs_0_, ...), custom_call_target="tpu_custom_call" | custom-call | tf_op jit(solution)/shard_map/cond/branch_2_fun/pallas_call | solution.py:358
  108.9 0.0 collective-permute-done.29.refs_3_
  108.9 0.0 collective-permute-done.28.refs_2_
  108.9 0.0 collective-permute-done.34.refs_13_
  108.9 17.8 %branch_2_fun.9 = bf16[384,5120]{1,0:T(8,128)(2,1)} custom-call(s32[8,20]{1,0:T(8,128)S(1)} %get-tuple-element.145.meta_ref, s32[8]{0:T(128)S(1)} %get-tuple-element.146.flag_ref, f32[2,96,96]{2,1,0:T(8,128)S(1)} %copy-done.6, bf16[5,1,384,128]{3,2,1,0:T(8,128)(2,1)} %get-tuple-element.165.refs_0_, bf16[5,2,384,128]{3,2,1,0:T(8,128)(2,1)} %get-tuple-element.166.refs_1_, ...), custom_call_target="tpu_custom_call" | custom-call | tf_op jit(solution)/shard_map/cond/branch_2_fun/pallas_call | solution.py:358
  (1 shorter events, 0.0 us)
Async XLA Ops:
  4.2 104.7 %collective-permute-start.34 = (bf16[1280,5120]{1,0:T(8,128)(2,1)}, bf16[1280,5120]{1,0:T(8,128)(2,1)}, u32[]{:S(2)}, u32[]{:S(2)}) collective-permute-start(bf16[1280,5120]{1,0:T(8,128)(2,1)} %get-tuple-element.179.refs_12_), channel_id=1, source_target_pairs={{0,1},{1,0},{2,3},{3,2},{4,5},{5,4},{6,7},{7,6},{8,9},{9,8},{10,11... | collective-permute-start | bytes 39321608 | tf_op jit(solution)/shard_map/cond/branch_2_fun/ppermute | solution.py:412
  4.9 16.0 %copy-start.2 = (bf16[384,2560]{1,0:T(8,128)(2,1)S(1)}, bf16[384,2560]{1,0:T(8,128)(2,1)}, u32[]{:S(2)}) copy-start(bf16[384,2560]{1,0:T(8,128)(2,1)} %get-tuple-element.150.refs_2_) | copy-start | bytes 5898244 | tf_op jit(solution)/shard_map/cond
  10.8 19.2 %collective-permute-start.24 = (bf16[14,2,96,128]{3,2,1,0:T(8,128)(2,1)}, bf16[14,2,96,128]{3,2,1,0:T(8,128)(2,1)}, u32[]{:S(2)}, u32[]{:S(2)}) collective-permute-start(bf16[14,2,96,128]{3,2,1,0:T(8,128)(2,1)} %get-tuple-element.152), channel_id=1, source_target_pairs={{0,2},{2,4},{4,6},{6,8},{8,10},{10,12},{12,14},{1,3},{3,5},{5,7},{... | collective-permute-start | bytes 2064392 | tf_op jit(solution)/shard_map/cond/branch_2_fun/ppermute | solution.py:391
  12.1 18.8 %collective-permute-start.25 = (bf16[14,2,96,128]{3,2,1,0:T(8,128)(2,1)}, bf16[14,2,96,128]{3,2,1,0:T(8,128)(2,1)}, u32[]{:S(2)}, u32[]{:S(2)}) collective-permute-start(bf16[14,2,96,128]{3,2,1,0:T(8,128)(2,1)} %get-tuple-element.153), channel_id=1, source_target_pairs={{2,0},{4,2},{6,4},{8,6},{10,8},{12,10},{14,12},{3,1},{5,3},{7,5},{... | collective-permute-start | bytes 2064392 | tf_op jit(solution)/shard_map/cond/branch_2_fun/ppermute | solution.py:391
  16.9 62.3 %collective-permute-start.31 = (bf16[8,2,384,128]{3,2,1,0:T(8,128)(2,1)}, bf16[8,2,384,128]{3,2,1,0:T(8,128)(2,1)}, u32[]{:S(2)}, u32[]{:S(2)}) collective-permute-start(bf16[8,2,384,128]{3,2,1,0:T(8,128)(2,1)} %get-tuple-element.168.refs_1_), channel_id=1, source_target_pairs={{1,16},{17,32},{33,48},{49,64},{65,80},{81,96},{97,112},{16,1},{32... | collective-permute-start | bytes 4718600 | tf_op jit(solution)/shard_map/cond/branch_2_fun/ppermute | solution.py:410
  20.8 60.9 %collective-permute-start.30 = (bf16[8,2,384,128]{3,2,1,0:T(8,128)(2,1)}, bf16[8,2,384,128]{3,2,1,0:T(8,128)(2,1)}, u32[]{:S(2)}, u32[]{:S(2)}) collective-permute-start(bf16[8,2,384,128]{3,2,1,0:T(8,128)(2,1)} %get-tuple-element.168.refs_1_), channel_id=1, source_target_pairs={{0,1},{1,0},{2,3},{3,2},{4,5},{5,4},{6,7},{7,6},{8,9},{9,8},{10,11... | collective-permute-start | bytes 4718600 | tf_op jit(solution)/shard_map/cond/branch_2_fun/ppermute | solution.py:411
  30.9 3.1 %collective-permute-start.26 = (bf16[14,2,96,128]{3,2,1,0:T(8,128)(2,1)}, bf16[14,2,96,128]{3,2,1,0:T(8,128)(2,1)S(1)}, u32[]{:S(2)}, u32[]{:S(2)}) collective-permute-start(bf16[14,2,96,128]{3,2,1,0:T(8,128)(2,1)} %collective-permute-done.24.refs_2_.refs_6_), channel_id=1, source_target_pairs={{0,1},{1,0},{2,3},{3,2},{4,5},{5,4},{6,7},{7,6},{8,9},{9,8},{10,11... | collective-permute-start | bytes 2064392 | tf_op jit(solution)/shard_map/cond/branch_2_fun/ppermute | solution.py:394
  32.0 5.7 %collective-permute-start.27 = (bf16[14,2,96,128]{3,2,1,0:T(8,128)(2,1)}, bf16[14,2,96,128]{3,2,1,0:T(8,128)(2,1)S(1)}, u32[]{:S(2)}, u32[]{:S(2)}) collective-permute-start(bf16[14,2,96,128]{3,2,1,0:T(8,128)(2,1)} %collective-permute-done.25.refs_3_.refs_7_), channel_id=1, source_target_pairs={{0,1},{1,0},{2,3},{3,2},{4,5},{5,4},{6,7},{7,6},{8,9},{9,8},{10,11... | collective-permute-start | bytes 2064392 | tf_op jit(solution)/shard_map/cond/branch_2_fun/ppermute | solution.py:394
  34.0 11.6 %copy-start.11 = (bf16[14,2,96,128]{3,2,1,0:T(8,128)(2,1)}, bf16[14,2,96,128]{3,2,1,0:T(8,128)(2,1)S(1)}, u32[]{:S(2)}) copy-start(bf16[14,2,96,128]{3,2,1,0:T(8,128)(2,1)S(1)} %collective-permute-done.26.refs_8_) | copy-start | bytes 2064388 | tf_op jit(solution)/shard_map/cond
  34.0 74.9 %collective-permute-start.29 = (bf16[5,2,384,128]{3,2,1,0:T(8,128)(2,1)}, bf16[5,2,384,128]{3,2,1,0:T(8,128)(2,1)}, u32[]{:S(2)}, u32[]{:S(2)}) collective-permute-start(bf16[5,2,384,128]{3,2,1,0:T(8,128)(2,1)} %get-tuple-element.166.refs_1_), channel_id=1, source_target_pairs={{1,16},{17,32},{33,48},{49,64},{65,80},{81,96},{97,112},{16,1},{32... | collective-permute-start | bytes 2949128 | tf_op jit(solution)/shard_map/cond/branch_2_fun/ppermute | solution.py:410
  37.7 7.9 %copy-start.12 = (bf16[14,2,96,128]{3,2,1,0:T(8,128)(2,1)}, bf16[14,2,96,128]{3,2,1,0:T(8,128)(2,1)S(1)}, u32[]{:S(2)}) copy-start(bf16[14,2,96,128]{3,2,1,0:T(8,128)(2,1)S(1)} %collective-permute-done.27.refs_9_) | copy-start | bytes 2064388 | tf_op jit(solution)/shard_map/cond
  37.7 71.2 %collective-permute-start.28 = (bf16[5,2,384,128]{3,2,1,0:T(8,128)(2,1)}, bf16[5,2,384,128]{3,2,1,0:T(8,128)(2,1)}, u32[]{:S(2)}, u32[]{:S(2)}) collective-permute-start(bf16[5,2,384,128]{3,2,1,0:T(8,128)(2,1)} %get-tuple-element.166.refs_1_), channel_id=1, source_target_pairs={{0,1},{1,0},{2,3},{3,2},{4,5},{5,4},{6,7},{7,6},{8,9},{9,8},{10,11... | collective-permute-start | bytes 2949128 | tf_op jit(solution)/shard_map/cond/branch_2_fun/ppermute | solution.py:411
  37.8 57.7 %copy-start.6 = (f32[2,96,96]{2,1,0:T(8,128)S(1)}, f32[2,96,96]{2,1,0:T(8,128)}, u32[]{:S(2)}) copy-start(f32[2,96,96]{2,1,0:T(8,128)} %get-tuple-element.147.mask_ref) | copy-start | bytes 221188 | tf_op jit(solution)/shard_map/cond
  80.4 10.1 %collective-permute-start.33 = (bf16[8,2,96,128]{3,2,1,0:T(8,128)(2,1)S(1)}, bf16[8,2,96,128]{3,2,1,0:T(8,128)(2,1)S(1)}, u32[]{:S(2)}, u32[]{:S(2)}) collective-permute-start(bf16[8,2,96,128]{3,2,1,0:T(8,128)(2,1)S(1)} %get-tuple-element.230), channel_id=1, source_target_pairs={{2,0},{4,2},{6,4},{8,6},{10,8},{12,10},{14,12},{3,1},{5,3},{7,5},{... | collective-permute-start | bytes 1179656 | tf_op jit(solution)/shard_map/cond/branch_2_fun/ppermute | solution.py:399
  81.8 13.0 %collective-permute-start.32 = (bf16[8,2,96,128]{3,2,1,0:T(8,128)(2,1)S(1)}, bf16[8,2,96,128]{3,2,1,0:T(8,128)(2,1)S(1)}, u32[]{:S(2)}, u32[]{:S(2)}) collective-permute-start(bf16[8,2,96,128]{3,2,1,0:T(8,128)(2,1)S(1)} %get-tuple-element.231), channel_id=1, source_target_pairs={{0,2},{2,4},{4,6},{6,8},{8,10},{10,12},{12,14},{1,3},{3,5},{5,7},{... | collective-permute-start | bytes 1179656 | tf_op jit(solution)/shard_map/cond/branch_2_fun/ppermute | solution.py:398
  90.5 4.2 %copy-start.17 = (bf16[8,2,96,128]{3,2,1,0:T(8,128)(2,1)}, bf16[8,2,96,128]{3,2,1,0:T(8,128)(2,1)S(1)}, u32[]{:S(2)}) copy-start(bf16[8,2,96,128]{3,2,1,0:T(8,128)(2,1)S(1)} %collective-permute-done.33.refs_5_) | copy-start | bytes 1179652 | tf_op jit(solution)/shard_map/cond
  94.8 0.8 copy-start.18
where the time goes:
time: 128 us; the launch traced here: 127 us
  Pallas kernels  52 us (41%)
  waiting for transfers between devices  51.9 us (41%)
  starting transfers between devices  18.4 us (14%)
  local copies, waits for them, and re-layouts  3.31 us (3%)
    pallas_call x3, Pallas kernels, chunk(): pl.pallas_call(kernel, out_shape=jax.ShapeDtypeStruct(shape, out_type), i...  38.9 us
    ppermute x2, waiting for transfers between devices, call(): beyond = [lax.ppermute(x, GRID_AXES, outer_pairs) for x in packed]  33.7 us
    pallas_call x2, Pallas kernels, pack_heads(): pl.pallas_call(kernel, out_shape=[jax.ShapeDtypeStruct(shape, sources[0]....  11.2 us
    ppermute x2, starting transfers between devices, call(): beyond = [lax.ppermute(x, GRID_AXES, outer_pairs) for x in packed]  7.57 us
    ppermute x1, waiting for transfers between devices, trade_corners(): lax.ppermute(beyond[:, :, :tile], 'height', up)  7.5 us
    ppermute x2, starting transfers between devices, trade_edges(): return (lax.ppermute(high, 'height', down), lax.ppermute(low, 'height', up))  6.16 us
    ppermute x2, waiting for transfers between devices, trade_edges(): return (lax.ppermute(high, 'height', down), lax.ppermute(low, 'height', up))  4.57 us
    ppermute x1, waiting for transfers between devices, trade_corners(): lax.ppermute(beyond[:, :, tokens - tile:], 'height', down)  4.21 us
  transfers between devices with their start and end apart: 11, of which 6 were waited for; matrix products, arithmetic and copies ran while one was open for 1% of the time, Pallas kernels for 25%

commit v1 on v0

--- a/solution.py
+++ b/solution.py
@@ -29,12 +29,12 @@
             both += rad_f * rad_r
             side += rad_f * (1 - rad_r)
             edge += (1 - rad_f) * rad_r
-        starts = [both + side + edge, both + side, both, 0]
+        starts = [both + side, heads - edge, both, 0]
         for head in range(heads):
             rad_f, rad_r = radii_ref[head, 0], radii_ref[head, 1]
             kind = 2 * rad_f + rad_r
             place = sum(jnp.where(kind == i, starts[i], 0) for i in range(4))
-            slot = place + jnp.where(kind == 2, edge, 0) - jnp.where(kind == 1, side, 0)
+            slot = place + jnp.where(kind == 1, both - (heads - edge), jnp.where(kind == 3, 0, edge))
             starts = [starts[i] + (kind == i).astype(jnp.int32) for i in range(4)]
             meta_ref[0, place] = head
             meta_ref[1, place] = rad_f
@@ -57,6 +57,7 @@
         level = jnp.int32(0)
         for i, (most_side, most_both, most_edge) in enumerate(levels):
             fits = (both + side <= most_side) & (both <= most_both) & (both + edge <= most_edge)
+            fits = fits & ((edge <= heads - most_side) | (most_side == heads))
             level = jnp.where(fits, i, level)
         level_ref[0] = level
 
@@ -135,14 +136,17 @@
     return (out.T if flip else out).astype(jnp.bfloat16)
 
 
-def chunk(meta, flags, col_masks, first, own, given, weights, block, tile, tiles, unroll=2):
+def chunk(meta, flags, col_masks, first, own, given, weights, total_in, last, tile, tiles, unroll=2):
     tokens = tile * tiles
-    count = own["query"].shape[0]
-    sides, corners, edges = own.get("sides", ()), own.get("corners", ()), own["edges"]
+    count = own["query"].shape[0] if own else 0
+    sides, corners = (own.get("sides", ()), own.get("corners", ())) if own else ((), ())
+    edges = own["edges"] if own else ()
     places = [(start + i, g, i) for g, (start, x) in enumerate(given) for i in range(x.shape[0])]
-    depth = weights[0].shape[0] if weights else 0
+    places += [(first + i, None, i) for i in range(count)]
+    depth = len(places)
     width = weights[0].shape[1] if weights else 0
-    blocks = width // block
+    blocks, parts = 4, 2
+    block, part_width = width // blocks, width // parts
     across = 1 + len(sides)
 
     def kernel(meta_ref, flag_ref, mask_ref, *refs):
@@ -151,15 +155,22 @@
         def take(items):
             return [refs.pop(0) for _ in items]
 
-        query_ref, pair_ref = take(range(2))
+        query_ref, pair_ref = take(range(2)) if own else (None, None)
         side_refs, corner_refs = take(sides), take(corners)
         edge_refs = take(edges)
         given_refs, weight_refs = take(given), take(weights)
+        total_ref = refs.pop(0) if total_in is not None else None
         out_ref = refs.pop(0)
-        query_buf, pair_buf, edge_buf, key_buf, value_buf, attended, own_sem, edge_sem = take(range(8))
+        if own:
+            query_buf, pair_buf, edge_buf, key_buf, value_buf, attended, own_sem, edge_sem = take(range(8))
         side_buf, corner_buf = take(sides[:1]), take(corners[:1])
+        given_bufs = take(given)
+        if given:
+            given_sem = refs.pop(0)
         if weights:
-            given_sem, weight_buf, weight_sem, out_buf, out_sem = take(range(5))
+            weight_buf, weight_sem, out_buf, out_sem = take(range(4))
+        if total_ref is not None:
+            total_buf, total_sem = take(range(2))
 
         def own_copies(at):
             pairs = [(query_ref.at[at], query_buf.at[at]), (pair_ref.at[at], pair_buf.at[at])]
@@ -178,36 +189,48 @@
                 copy.start()
             slot = meta_ref[4, first + at]
 
-            for copy in edge_copies(at, jnp.minimum(slot, edges[0].shape[0] - 1)):
-                copy.start()
+            if edges:
+                for copy in edge_copies(at, jnp.minimum(slot, edges[0].shape[0] - 1)):
+                    copy.start()
 
             return carry
 
-        def head_columns(place):
-            half = jnp.where(meta_ref[5, place] == flag_ref[4], 0, depth)
-            return pl.ds(pl.multiple_of(half + meta_ref[6, place] * HEAD_DIM, HEAD_DIM), HEAD_DIM)
-
-        def given_copy(index):
-            place, g, i = places[index]
-            return pltpu.make_async_copy(
-                given_refs[g].at[i], attended.at[:, head_columns(place)], given_sem.at[index]
-            )
+        def given_copy(g):
+            return pltpu.make_async_copy(given_refs[g], given_bufs[g], given_sem.at[g])
 
         def columns(at):
             return pl.ds(pl.multiple_of(at * block, block), block)
 
-        def weight_copies(at):
-            return [
-                pltpu.make_async_copy(x.at[:, columns(at)], weight_buf.at[i, :, columns(at)], weight_sem.at[i, at])
-                for i, x in enumerate(weight_refs)
-            ]
+        def weight_copy(index, part, source):
+            row = pl.multiple_of(meta_ref[6, places[index][0]] * HEAD_DIM, HEAD_DIM)
+            wide = pl.ds(pl.multiple_of(part * part_width, part_width), part_width)
+            return pltpu.make_async_copy(
+                source.at[pl.ds(row, HEAD_DIM), wide],
+                weight_buf.at[pl.ds(index * HEAD_DIM, HEAD_DIM), wide],
+                weight_sem.at[index, part],
+            )
+
+        def total_copy(at):
+            return pltpu.make_async_copy(total_ref.at[:, columns(at)], total_buf.at[:, columns(at)], total_sem.at[at])
 
         def out_copy(at):
             return pltpu.make_async_copy(out_buf.at[:, columns(at)], out_ref.at[:, columns(at)], out_sem.at[at])
 
-        def begin_share(at, carry):
-            for copy in weight_copies(at):
-                copy.start()
+        def begin_share(part, carry):
+            for index in range(depth):
+                mine = meta_ref[5, places[index][0]] == flag_ref[4]
+
+                @pl.when(mine)
+                def _():
+                    weight_copy(index, part, weight_refs[0]).start()
+
+                @pl.when(jnp.logical_not(mine))
+                def _():
+                    weight_copy(index, part, weight_refs[1]).start()
+
+            if total_ref is not None:
+                for at in range(blocks // parts):
+                    total_copy(part * (blocks // parts) + at).start()
             return carry
 
         def tile_rows(at, size=1):
@@ -236,13 +259,9 @@
 
             def run(at, start, biases, flip):
                 rows, held = tile_rows(at), tile_rows(start, len(biases))
-                found = attend(
+                attended[head, rows, :] = attend(
                     query_buf[head, 0, rows, :], key_buf[held, :], value_buf[held, :], col_mask, biases, flip
                 )
-                if weights:
-                    attended[rows, head_columns(place)] = found
-                else:
-                    attended[head, rows, :] = found
 
             def fill(band):
                 def step(at, carry):
@@ -273,9 +292,10 @@
                 lax.fori_loop(0, tiles, each, 0, unroll=tiles if across == 1 else unroll)
 
             if sides:
-                pl.when(rad_r > 0)(with_rows)
-
-                @pl.when(rad_r == 0)
+                if edges:
+                    pl.when(rad_r > 0)(with_rows)
+
+                @pl.when((rad_r == 0) if edges else True)
                 def _():
                     fill(0)
 
@@ -289,35 +309,40 @@
                 with_rows()
             return carry
 
-        def share(at, carry):
-            for copy in weight_copies(at):
-                copy.wait()
-            total = sum(
-                jnp.dot(
-                    attended[:, i * depth : (i + 1) * depth], weight_buf[i, :, columns(at)],
-                    preferred_element_type=jnp.float32,
-                )
-                for i in range(2)
-            )
-            out_buf[:, columns(at)] = total.astype(out_buf.dtype)
-            out_copy(at).start()
-            return carry
+        def share(part, carry):
+            for index in range(depth):
+                weight_copy(index, part, weight_refs[0]).wait()
+
+            def each(i, carry):
+                at = part * (blocks // parts) + i
+                held = [attended[i] if g is None else given_bufs[g][i] for _, g, i in places]
+                left = jnp.concatenate(held, axis=1)
+                total = jnp.dot(left, weight_buf[:, columns(at)], preferred_element_type=jnp.float32)
+                if total_ref is not None:
+                    total_copy(at).wait()
+                    total += total_buf[:, columns(at)]
+                out_buf[:, columns(at)] = total.astype(out_buf.dtype)
+                out_copy(at).start()
+                return carry
+
+            return lax.fori_loop(0, blocks // parts, each, carry)
 
         def end_share(at, carry):
             out_copy(at).wait()
             return carry
 
-        lax.fori_loop(0, count, begin_own, 0)
+        if own:
+            lax.fori_loop(0, count, begin_own, 0)
+        for g in range(len(given)):
+            given_copy(g).start()
         if weights:
-            for index in range(len(places)):
-                given_copy(index).start()
-            lax.fori_loop(0, blocks, begin_share, 0)
-        lax.fori_loop(0, count, head_step, 0)
+            lax.fori_loop(0, parts, begin_share, 0)
+        if own:
+            lax.fori_loop(0, count, head_step, 0)
+        for g in range(len(given)):
+            given_copy(g).wait()
         if weights:
-            for index in range(len(places)):
-                given_copy(index).wait()
-        if weights:
-            lax.fori_loop(0, blocks, share, 0)
+            lax.fori_loop(0, parts, share, 0)
             lax.fori_loop(0, blocks, end_share, 0)
         else:
             done = pltpu.make_async_copy(attended, out_ref, own_sem.at[0, 0])
@@ -327,33 +352,39 @@
     anywhere, smem = pl.BlockSpec(memory_space=pl.ANY), pl.BlockSpec(memory_space=pltpu.SMEM)
     operands, scratch = [], []
     bf16 = jnp.bfloat16
-    operands += [own["query"], own["pair"], *sides, *corners, *edges]
-    kinds = 2 + len(sides) + len(corners)
-    scratch += [
+    if own:
+        operands += [own["query"], own["pair"], *sides, *corners, *edges]
+        kinds = 2 + len(sides) + len(corners)
+        scratch += [
             pltpu.VMEM(own["query"].shape, bf16),
             pltpu.VMEM(own["pair"].shape, bf16),
-            pltpu.VMEM((count, len(edges), 2, tile, HEAD_DIM), bf16),
+            pltpu.VMEM((count, max(len(edges), 1), 2, tile, HEAD_DIM), bf16),
             pltpu.VMEM((across * (tiles + 2) * tile, HEAD_DIM), bf16),
             pltpu.VMEM((across * (tiles + 2) * tile, HEAD_DIM), bf16),
-            pltpu.VMEM((tokens, 2 * depth) if weights else (count, tokens, HEAD_DIM), bf16),
+            pltpu.VMEM((count, tokens, HEAD_DIM), bf16),
             pltpu.SemaphoreType.DMA((count, kinds)),
-            pltpu.SemaphoreType.DMA((count, len(edges))),
+            pltpu.SemaphoreType.DMA((count, max(len(edges), 1))),
         ]
     if sides:
         scratch.append(pltpu.VMEM((count, 2, 2, tokens, HEAD_DIM), bf16))
     if corners:
         scratch.append(pltpu.VMEM((count, 2, 2, tile, HEAD_DIM), bf16))
     operands += [x for _, x in given]
-    out_type = bf16
+    scratch += [pltpu.VMEM(x.shape, bf16) for _, x in given]
+    if given:
+        scratch.append(pltpu.SemaphoreType.DMA((len(given),)))
+    out_type = bf16 if last or not weights else jnp.float32
     if weights:
         operands += list(weights)
         scratch += [
-            pltpu.SemaphoreType.DMA((len(places),)),
-            pltpu.VMEM((2, depth, width), bf16),
-            pltpu.SemaphoreType.DMA((2, blocks)),
+            pltpu.VMEM((depth * HEAD_DIM, width), bf16),
+            pltpu.SemaphoreType.DMA((depth, parts)),
             pltpu.VMEM((tokens, width), out_type),
             pltpu.SemaphoreType.DMA((blocks,)),
         ]
+    if total_in is not None:
+        operands.append(total_in)
+        scratch += [pltpu.VMEM((tokens, width), jnp.float32), pltpu.SemaphoreType.DMA((blocks,))]
     shape = (tokens, width) if weights else (count, tokens, HEAD_DIM)
     return pl.pallas_call(
         kernel,
@@ -422,18 +453,21 @@
             near = beyond[0]
             if rest:
                 own = {"query": ordered[2], "pair": ordered[3], "edges": edges[:2]}
-                lone = chunk(*common, side_count, own, [], (), 1024, tile, tiles)
+                lone = chunk(*common, side_count, own, [], (), None, False, tile, tiles)
                 near, lone = lax.optimization_barrier((near, lone))
-                shared.append((side_count, lone))
             corners = trade_corners(near)
+            total = None
+            if rest:
+                total = chunk(*common, 0, None, [(side_count, lone)], weights, None, False, tile, tiles)
+                corners, total = lax.optimization_barrier((corners, total))
             own = {"query": ordered[0], "pair": packed[0], "sides": (beside[0], near), "edges": edges, "corners": corners}
-            first = chunk(*common, 0, own, [], (), 1024, tile, tiles, 4)
+            first = chunk(*common, 0, own, [], (), None, False, tile, tiles, 4)
             far, first = lax.optimization_barrier((beyond[1], first))
             shared.append((0, first))
+            own = {"query": ordered[1], "pair": packed[1], "sides": (beside[1], far), "edges": ()}
             if both_count > size:
-                corners = trade_corners(far)
-            own = {"query": ordered[1], "pair": packed[1], "sides": (beside[1], far), "edges": edges, "corners": corners}
-            return chunk(*common, size, own, shared, weights, 1024, tile, tiles)
+                own.update({"edges": edges, "corners": trade_corners(far)})
+            return chunk(*common, size, own, shared, weights, total, True, tile, tiles)
 
         return call
 

time: 128 us -> 128 us (level)
  the two profiles are of different devices: /device:TPU:95 before, /device:TPU:54 now
where the time goes in v1:
time: 128 us; the launch traced here: 127 us
  Pallas kernels  58.7 us (46%)
  waiting for transfers between devices  42.5 us (33%)
  starting transfers between devices  19.5 us (15%)
  local copies, waits for them, and re-layouts  4.74 us (4%)
    pallas_call x4, Pallas kernels, chunk(): pl.pallas_call(kernel, out_shape=jax.ShapeDtypeStruct(shape, out_type), i...  45.5 us
    ppermute x2, waiting for transfers between devices, call(): beyond = [lax.ppermute(x, GRID_AXES, outer_pairs) for x in packed]  33.7 us
    pallas_call x2, Pallas kernels, pack_heads(): pl.pallas_call(kernel, out_shape=[jax.ShapeDtypeStruct(shape, sources[0]....  11.3 us
    ppermute x2, waiting for transfers between devices, trade_edges(): return (lax.ppermute(high, 'height', down), lax.ppermute(low, 'height', up))  6.87 us
    ppermute x2, starting transfers between devices, trade_edges(): return (lax.ppermute(high, 'height', down), lax.ppermute(low, 'height', up))  6.71 us
    ppermute x1, starting transfers between devices, trade_corners(): lax.ppermute(beyond[:, :, :tile], 'height', up)  5.32 us
    ppermute x2, starting transfers between devices, call(): beyond = [lax.ppermute(x, GRID_AXES, outer_pairs) for x in packed]  4.72 us
  transfers between devices with their start and end apart: 11, of which 4 were waited for; matrix products, arithmetic and copies ran while one was open for 2% of the time, Pallas kernels for 32%

profile of v1, /device:TPU:54, one launch (start us, length us, event | category | flops | bytes accessed | tf_op | source)
XLA Modules:
  0.0 127.0 jit_solution(16981431340968012681)
XLA Ops:
  0.0 1.4 %copy.12.radii_ref = s32[20,3]{1,0:T(8,128)} copy(s32[20,3]{0,1:T(4,128)} %param.15) | data formatting | bytes 480 | tf_op args[4]
  1.4 1.9 %shard_map.77 = (s32[8,20]{1,0:T(8,128)S(1)}, s32[20]{0:T(128)S(1)}, s32[8]{0:T(128)S(1)}, s32[1]{0:T(128)}) custom-call(s32[20,3]{1,0:T(8,128)} %copy.12.radii_ref, s32[16]{0:T(128)} %valid_ref.1), custom_call_target="tpu_custom_call" | custom-call | tf_op jit(solution)/shard_map/pallas_call | solution.py:66
  3.9 122.8 %conditional.1 = (bf16[1,8,48,5120]{3,2,1,0:T(8,128)(2,1)}) conditional(s32[]{:T(128)} %bitcast.4, (s32[20]{0:T(128)S(1)}, s32[20]{0:T(128)S(1)}, bf16[384,2560]{1,0:T(8,128)(2,1)}, bf16[384,2560]{1,0:T(8,128)(2,1)}, bf16[384,2560]{1,0:T(8,128)(2,1)}, /*index=5*/s32[8,20]{1,0:T(8,128)S(1)}, s32[8]{0:T(128)S(1)}, ...), branch_computations={%region_0.0_spmd, %region_1.0_spmd, %region_2.0_spmd, %region_3.0_... | conditional | bytes 129401536 | solution.py:474
  4.2 0.1 collective-permute-start.34
  4.3 0.0 copy-start.2
  4.3 5.9 %branch_2_fun.6 = (bf16[8,2,384,128]{3,2,1,0:T(8,128)(2,1)}, bf16[5,2,384,128]{3,2,1,0:T(8,128)(2,1)}, bf16[14,2,96,128]{3,2,1,0:T(8,128)(2,1)}, bf16[14,2,96,128]{3,2,1,0:T(8,128)(2,1)}) custom-call(s32[20]{0:T(128)S(1)} %get-tuple-element.151.refs_0_, s32[20]{0:T(128)S(1)} %get-tuple-element.152.refs_1_, bf16[384,2560]{1,0:T(8,128)(2,1)} %get-tuple-element.153.refs_2_, ...), custom_call_target="tpu_custom_call" | custom-call | tf_op jit(solution)/shard_map/cond/branch_2_fun/pallas_call | solution.py:113
  10.2 1.3 %collective-permute-start.24 = (bf16[14,2,96,128]{3,2,1,0:T(8,128)(2,1)}, bf16[14,2,96,128]{3,2,1,0:T(8,128)(2,1)}, u32[]{:S(2)}, u32[]{:S(2)}) collective-permute-start(bf16[14,2,96,128]{3,2,1,0:T(8,128)(2,1)} %get-tuple-element.155), channel_id=1, source_target_pairs={{0,2},{2,4},{4,6},{6,8},{8,10},{10,12},{12,14},{1,3},{3,5},{5,7},{... | collective-permute-start | bytes 2064392 | tf_op jit(solution)/shard_map/cond/branch_2_fun/ppermute | solution.py:422
  11.5 5.4 %collective-permute-start.25 = (bf16[14,2,96,128]{3,2,1,0:T(8,128)(2,1)}, bf16[14,2,96,128]{3,2,1,0:T(8,128)(2,1)}, u32[]{:S(2)}, u32[]{:S(2)}) collective-permute-start(bf16[14,2,96,128]{3,2,1,0:T(8,128)(2,1)} %get-tuple-element.156), channel_id=1, source_target_pairs={{2,0},{4,2},{6,4},{8,6},{10,8},{12,10},{14,12},{3,1},{5,3},{7,5},{... | collective-permute-start | bytes 2064392 | tf_op jit(solution)/shard_map/cond/branch_2_fun/ppermute | solution.py:422
  16.9 2.3 %collective-permute-start.31 = (bf16[8,2,384,128]{3,2,1,0:T(8,128)(2,1)}, bf16[8,2,384,128]{3,2,1,0:T(8,128)(2,1)}, u32[]{:S(2)}, u32[]{:S(2)}) collective-permute-start(bf16[8,2,384,128]{3,2,1,0:T(8,128)(2,1)} %get-tuple-element.171.refs_1_), channel_id=1, source_target_pairs={{1,16},{17,32},{33,48},{49,64},{65,80},{81,96},{97,112},{16,1},{32... | collective-permute-start | bytes 4718600 | tf_op jit(solution)/shard_map/cond/branch_2_fun/ppermute | solution.py:441
  19.2 0.0 copy-done.2
  19.2 5.4 %branch_2_fun.7 = (bf16[8,1,384,128]{3,2,1,0:T(8,128)(2,1)}, bf16[5,1,384,128]{3,2,1,0:T(8,128)(2,1)}, bf16[7,1,384,128]{3,2,1,0:T(8,128)(2,1)}, bf16[7,2,384,128]{3,2,1,0:T(8,128)(2,1)}) custom-call(s32[20]{0:T(128)S(1)} %get-tuple-element.151.refs_0_, bf16[384,2560]{1,0:T(8,128)(2,1)} %get-tuple-element.157.refs_1_, bf16[384,2560]{1,0:T(8,128)(2,1)S(1)} %copy-done.2, ...), custom_call_target="tpu_custom_call" | custom-call | tf_op jit(solution)/shard_map/cond/branch_2_fun/pallas_call | solution.py:113
  24.5 5.7 %collective-permute-done.24.refs_2_.refs_6_ = bf16[14,2,96,128]{3,2,1,0:T(8,128)(2,1)} collective-permute-done((bf16[14,2,96,128]{3,2,1,0:T(8,128)(2,1)}, bf16[14,2,96,128]{3,2,1,0:T(8,128)(2,1)}, u32[]{:S(2)}, u32[]{:S(2)}) %collective-permute-start.24) | collective-permute-done | bytes 688160 | tf_op jit(solution)/shard_map/cond/branch_2_fun/ppermute | solution.py:422
  30.2 1.2 collective-permute-done.25.refs_3_.refs_7_
  31.4 0.0 collective-permute-start.26
  31.4 0.5 collective-permute-start.27
  31.9 0.0 collective-permute-start.30
  31.9 1.8 %collective-permute-done.26.refs_8_ = bf16[14,2,96,128]{3,2,1,0:T(8,128)(2,1)S(1)} collective-permute-done((bf16[14,2,96,128]{3,2,1,0:T(8,128)(2,1)}, bf16[14,2,96,128]{3,2,1,0:T(8,128)(2,1)S(1)}, u32[]{:S(2)}, u32[]{:S(2)}) %collective-permute-start.26) | collective-permute-done | bytes 688160 | tf_op jit(solution)/shard_map/cond/branch_2_fun/ppermute | solution.py:425
  33.8 0.0 copy-start.14
  33.8 2.5 %collective-permute-start.29 = (bf16[5,2,384,128]{3,2,1,0:T(8,128)(2,1)}, bf16[5,2,384,128]{3,2,1,0:T(8,128)(2,1)}, u32[]{:S(2)}, u32[]{:S(2)}) collective-permute-start(bf16[5,2,384,128]{3,2,1,0:T(8,128)(2,1)} %get-tuple-element.169.refs_1_), channel_id=1, source_target_pairs={{1,16},{17,32},{33,48},{49,64},{65,80},{81,96},{97,112},{16,1},{32... | collective-permute-start | bytes 2949128 | tf_op jit(solution)/shard_map/cond/branch_2_fun/ppermute | solution.py:441
  36.2 0.0 collective-permute-done.27.refs_9_
  36.2 0.0 copy-start.15
  36.3 0.9 collective-permute-start.28
  37.2 0.0 copy-done.14
  37.2 0.0 copy-done.15
  37.2 0.0 copy-start.6
  37.2 7.5 %branch_2_fun.8.refs_0_ = bf16[7,384,128]{2,1,0:T(8,128)(2,1)} custom-call(s32[8,20]{1,0:T(8,128)S(1)} %get-tuple-element.148.meta_ref, s32[8]{0:T(128)S(1)} %get-tuple-element.149.flag_ref, f32[2,96,96]{2,1,0:T(8,128)} %get-tuple-element.150.mask_ref, bf16[7,1,384,128]{3,2,1,0:T(8,128)(2,1)} %get-tuple-element.172.refs_0_, ...), custom_call_target="tpu_custom_call" | custom-call | tf_op jit(solution)/shard_map/cond/branch_2_fun/pallas_call | solution.py:389
  44.7 33.7 %collective-permute-done.31.refs_3_ = bf16[8,2,384,128]{3,2,1,0:T(8,128)(2,1)} collective-permute-done((bf16[8,2,384,128]{3,2,1,0:T(8,128)(2,1)}, bf16[8,2,384,128]{3,2,1,0:T(8,128)(2,1)}, u32[]{:S(2)}, u32[]{:S(2)}) %collective-permute-start.31) | collective-permute-done | bytes 1572896 | tf_op jit(solution)/shard_map/cond/branch_2_fun/ppermute | solution.py:441
  78.4 2.1 %fusion.3 = (bf16[8,2,96,128]{3,2,1,0:T(8,128)(2,1)}, bf16[8,2,96,128]{3,2,1,0:T(8,128)(2,1)}) fusion(bf16[8,2,384,128]{3,2,1,0:T(8,128)(2,1)} %collective-permute-done.31.refs_3_), kind=kLoop, calls=%fused_computation.4 | loop fusion | bytes 1572864 | tf_op jit(solution)/shard_map/cond/branch_2_fun/slice | solution.py:430
  80.6 1.3 %collective-permute-start.32 = (bf16[8,2,96,128]{3,2,1,0:T(8,128)(2,1)}, bf16[8,2,96,128]{3,2,1,0:T(8,128)(2,1)}, u32[]{:S(2)}, u32[]{:S(2)}) collective-permute-start(bf16[8,2,96,128]{3,2,1,0:T(8,128)(2,1)} %get-tuple-element.240), channel_id=1, source_target_pairs={{0,2},{2,4},{4,6},{6,8},{8,10},{10,12},{12,14},{1,3},{3,5},{5,7},{... | collective-permute-start | bytes 1179656 | tf_op jit(solution)/shard_map/cond/branch_2_fun/ppermute | solution.py:429
  81.9 0.0 collective-permute-done.34.refs_2_.refs_6_
  81.9 5.3 %collective-permute-start.33 = (bf16[8,2,96,128]{3,2,1,0:T(8,128)(2,1)}, bf16[8,2,96,128]{3,2,1,0:T(8,128)(2,1)}, u32[]{:S(2)}, u32[]{:S(2)}) collective-permute-start(bf16[8,2,96,128]{3,2,1,0:T(8,128)(2,1)} %get-tuple-element.239), channel_id=1, source_target_pairs={{2,0},{4,2},{6,4},{8,6},{10,8},{12,10},{14,12},{3,1},{5,3},{7,5},{... | collective-permute-start | bytes 1179656 | tf_op jit(solution)/shard_map/cond/branch_2_fun/ppermute | solution.py:430
  87.2 0.0 copy-done.6
  87.2 9.4 %branch_2_fun.9.refs_7_ = f32[384,5120]{1,0:T(8,128)} custom-call(s32[8,20]{1,0:T(8,128)S(1)} %get-tuple-element.148.meta_ref, s32[8]{0:T(128)S(1)} %get-tuple-element.149.flag_ref, f32[2,96,96]{2,1,0:T(8,128)S(1)} %copy-done.6, bf16[7,384,128]{2,1,0:T(8,128)(2,1)} %branch_2_fun.8.refs_0_, bf16[1280,5120]{1,0:T(8,128)(2,1)} %get-tuple-element.178.refs_1_.refs_5_, ...), custom_call_target="tpu_custom_call" | custom-call | tf_op jit(solution)/shard_map/cond/branch_2_fun/pallas_call | solution.py:389
  96.6 0.0 collective-permute-done.32.refs_4_
  96.6 0.0 collective-permute-done.33.refs_5_
  96.6 0.0 collective-permute-done.30.refs_2_
  96.7 0.0 copy-start.9
  96.7 1.2 copy-done.9
  97.9 12.1 %branch_2_fun.10.refs_4_ = bf16[8,384,128]{2,1,0:T(8,128)(2,1)} custom-call(s32[8,20]{1,0:T(8,128)S(1)} %get-tuple-element.148.meta_ref, s32[8]{0:T(128)S(1)} %get-tuple-element.149.flag_ref, f32[2,96,96]{2,1,0:T(8,128)S(1)} %copy-done.6, bf16[8,1,384,128]{3,2,1,0:T(8,128)(2,1)} %get-tuple-element.170.refs_0_, ...), custom_call_target="tpu_custom_call" | custom-call | tf_op jit(solution)/shard_map/cond/branch_2_fun/pallas_call | solution.py:389
  110.0 0.0 collective-permute-done.29.refs_3_
  110.0 0.0 collective-permute-done.28.refs_2_
  110.0 16.5 %branch_2_fun.11 = bf16[384,5120]{1,0:T(8,128)(2,1)} custom-call(s32[8,20]{1,0:T(8,128)S(1)} %get-tuple-element.148.meta_ref, s32[8]{0:T(128)S(1)} %get-tuple-element.149.flag_ref, f32[2,96,96]{2,1,0:T(8,128)S(1)} %copy-done.6, bf16[5,1,384,128]{3,2,1,0:T(8,128)(2,1)} %get-tuple-element.168.refs_0_, bf16[5,2,384,128]{3,2,1,0:T(8,128)(2,1)} %get-tuple-element.169.refs_1_, ...), custom_call_target="tpu_custom_call" | custom-call | tf_op jit(solution)/shard_map/cond/branch_2_fun/pallas_call | solution.py:389
  (1 shorter events, 0.0 us)
Async XLA Ops:
  4.2 77.7 %collective-permute-start.34 = (bf16[1280,5120]{1,0:T(8,128)(2,1)}, bf16[1280,5120]{1,0:T(8,128)(2,1)}, u32[]{:S(2)}, u32[]{:S(2)}) collective-permute-start(bf16[1280,5120]{1,0:T(8,128)(2,1)} %get-tuple-element.178.refs_1_.refs_5_), channel_id=1, source_target_pairs={{0,1},{1,0},{2,3},{3,2},{4,5},{5,4},{6,7},{7,6},{8,9},{9,8},{10,11... | collective-permute-start | bytes 39321608 | tf_op jit(solution)/shard_map/cond/branch_2_fun/ppermute | solution.py:443
  4.3 14.9 %copy-start.2 = (bf16[384,2560]{1,0:T(8,128)(2,1)S(1)}, bf16[384,2560]{1,0:T(8,128)(2,1)}, u32[]{:S(2)}) copy-start(bf16[384,2560]{1,0:T(8,128)(2,1)} %get-tuple-element.153.refs_2_) | copy-start | bytes 5898244 | tf_op jit(solution)/shard_map/cond
  10.2 20.0 %collective-permute-start.24 = (bf16[14,2,96,128]{3,2,1,0:T(8,128)(2,1)}, bf16[14,2,96,128]{3,2,1,0:T(8,128)(2,1)}, u32[]{:S(2)}, u32[]{:S(2)}) collective-permute-start(bf16[14,2,96,128]{3,2,1,0:T(8,128)(2,1)} %get-tuple-element.155), channel_id=1, source_target_pairs={{0,2},{2,4},{4,6},{6,8},{8,10},{10,12},{12,14},{1,3},{3,5},{5,7},{... | collective-permute-start | bytes 2064392 | tf_op jit(solution)/shard_map/cond/branch_2_fun/ppermute | solution.py:422
  11.5 19.9 %collective-permute-start.25 = (bf16[14,2,96,128]{3,2,1,0:T(8,128)(2,1)}, bf16[14,2,96,128]{3,2,1,0:T(8,128)(2,1)}, u32[]{:S(2)}, u32[]{:S(2)}) collective-permute-start(bf16[14,2,96,128]{3,2,1,0:T(8,128)(2,1)} %get-tuple-element.156), channel_id=1, source_target_pairs={{2,0},{4,2},{6,4},{8,6},{10,8},{12,10},{14,12},{3,1},{5,3},{7,5},{... | collective-permute-start | bytes 2064392 | tf_op jit(solution)/shard_map/cond/branch_2_fun/ppermute | solution.py:422
  16.9 61.5 %collective-permute-start.31 = (bf16[8,2,384,128]{3,2,1,0:T(8,128)(2,1)}, bf16[8,2,384,128]{3,2,1,0:T(8,128)(2,1)}, u32[]{:S(2)}, u32[]{:S(2)}) collective-permute-start(bf16[8,2,384,128]{3,2,1,0:T(8,128)(2,1)} %get-tuple-element.171.refs_1_), channel_id=1, source_target_pairs={{1,16},{17,32},{33,48},{49,64},{65,80},{81,96},{97,112},{16,1},{32... | collective-permute-start | bytes 4718600 | tf_op jit(solution)/shard_map/cond/branch_2_fun/ppermute | solution.py:441
  31.4 2.4 %collective-permute-start.26 = (bf16[14,2,96,128]{3,2,1,0:T(8,128)(2,1)}, bf16[14,2,96,128]{3,2,1,0:T(8,128)(2,1)S(1)}, u32[]{:S(2)}, u32[]{:S(2)}) collective-permute-start(bf16[14,2,96,128]{3,2,1,0:T(8,128)(2,1)} %collective-permute-done.24.refs_2_.refs_6_), channel_id=1, source_target_pairs={{0,1},{1,0},{2,3},{3,2},{4,5},{5,4},{6,7},{7,6},{8,9},{9,8},{10,11... | collective-permute-start | bytes 2064392 | tf_op jit(solution)/shard_map/cond/branch_2_fun/ppermute | solution.py:425
  31.4 4.8 %collective-permute-start.27 = (bf16[14,2,96,128]{3,2,1,0:T(8,128)(2,1)}, bf16[14,2,96,128]{3,2,1,0:T(8,128)(2,1)S(1)}, u32[]{:S(2)}, u32[]{:S(2)}) collective-permute-start(bf16[14,2,96,128]{3,2,1,0:T(8,128)(2,1)} %collective-permute-done.25.refs_3_.refs_7_), channel_id=1, source_target_pairs={{0,1},{1,0},{2,3},{3,2},{4,5},{5,4},{6,7},{7,6},{8,9},{9,8},{10,11... | collective-permute-start | bytes 2064392 | tf_op jit(solution)/shard_map/cond/branch_2_fun/ppermute | solution.py:425
  31.9 64.7 %collective-permute-start.30 = (bf16[8,2,384,128]{3,2,1,0:T(8,128)(2,1)}, bf16[8,2,384,128]{3,2,1,0:T(8,128)(2,1)S(1)}, u32[]{:S(2)}, u32[]{:S(2)}) collective-permute-start(bf16[8,2,384,128]{3,2,1,0:T(8,128)(2,1)} %get-tuple-element.171.refs_1_), channel_id=1, source_target_pairs={{0,1},{1,0},{2,3},{3,2},{4,5},{5,4},{6,7},{7,6},{8,9},{9,8},{10,11... | collective-permute-start | bytes 4718600 | tf_op jit(solution)/shard_map/cond/branch_2_fun/ppermute | solution.py:442
  33.8 3.4 %copy-start.14 = (bf16[14,2,96,128]{3,2,1,0:T(8,128)(2,1)}, bf16[14,2,96,128]{3,2,1,0:T(8,128)(2,1)S(1)}, u32[]{:S(2)}) copy-start(bf16[14,2,96,128]{3,2,1,0:T(8,128)(2,1)S(1)} %collective-permute-done.26.refs_8_) | copy-start | bytes 2064388 | tf_op jit(solution)/shard_map/cond
  33.8 76.2 %collective-permute-start.29 = (bf16[5,2,384,128]{3,2,1,0:T(8,128)(2,1)}, bf16[5,2,384,128]{3,2,1,0:T(8,128)(2,1)}, u32[]{:S(2)}, u32[]{:S(2)}) collective-permute-start(bf16[5,2,384,128]{3,2,1,0:T(8,128)(2,1)} %get-tuple-element.169.refs_1_), channel_id=1, source_target_pairs={{1,16},{17,32},{33,48},{49,64},{65,80},{81,96},{97,112},{16,1},{32... | collective-permute-start | bytes 2949128 | tf_op jit(solution)/shard_map/cond/branch_2_fun/ppermute | solution.py:441
  36.2 0.9 copy-start.15
  36.3 73.7 %collective-permute-start.28 = (bf16[5,2,384,128]{3,2,1,0:T(8,128)(2,1)}, bf16[5,2,384,128]{3,2,1,0:T(8,128)(2,1)}, u32[]{:S(2)}, u32[]{:S(2)}) collective-permute-start(bf16[5,2,384,128]{3,2,1,0:T(8,128)(2,1)} %get-tuple-element.169.refs_1_), channel_id=1, source_target_pairs={{0,1},{1,0},{2,3},{3,2},{4,5},{5,4},{6,7},{7,6},{8,9},{9,8},{10,11... | collective-permute-start | bytes 2949128 | tf_op jit(solution)/shard_map/cond/branch_2_fun/ppermute | solution.py:442
  37.2 50.0 %copy-start.6 = (f32[2,96,96]{2,1,0:T(8,128)S(1)}, f32[2,96,96]{2,1,0:T(8,128)}, u32[]{:S(2)}) copy-start(f32[2,96,96]{2,1,0:T(8,128)} %get-tuple-element.150.mask_ref) | copy-start | bytes 221188 | tf_op jit(solution)/shard_map/cond
  80.6 16.0 %collective-permute-start.32 = (bf16[8,2,96,128]{3,2,1,0:T(8,128)(2,1)}, bf16[8,2,96,128]{3,2,1,0:T(8,128)(2,1)}, u32[]{:S(2)}, u32[]{:S(2)}) collective-permute-start(bf16[8,2,96,128]{3,2,1,0:T(8,128)(2,1)} %get-tuple-element.240), channel_id=1, source_target_pairs={{0,2},{2,4},{4,6},{6,8},{8,10},{10,12},{12,14},{1,3},{3,5},{5,7},{... | collective-permute-start | bytes 1179656 | tf_op jit(solution)/shard_map/cond/branch_2_fun/ppermute | solution.py:429
  81.9 14.8 %collective-permute-start.33 = (bf16[8,2,96,128]{3,2,1,0:T(8,128)(2,1)}, bf16[8,2,96,128]{3,2,1,0:T(8,128)(2,1)}, u32[]{:S(2)}, u32[]{:S(2)}) collective-permute-start(bf16[8,2,96,128]{3,2,1,0:T(8,128)(2,1)} %get-tuple-element.239), channel_id=1, source_target_pairs={{2,0},{4,2},{6,4},{8,6},{10,8},{12,10},{14,12},{3,1},{5,3},{7,5},{... | collective-permute-start | bytes 1179656 | tf_op jit(solution)/shard_map/cond/branch_2_fun/ppermute | solution.py:430
  96.7 1.2 copy-start.9

commit v2 on v1

--- a/solution.py
+++ b/solution.py
@@ -19,19 +19,19 @@
 
 
 def plan_heads(window_radii, frame_valid, levels):
-    heads = window_radii.shape[0]
+    heads = window_radii.shape[1]
     frames = frame_valid.shape[0]
 
     def kernel(radii_ref, valid_ref, meta_ref, slot_ref, flag_ref, level_ref):
         both, side, edge = (jnp.int32(0) for _ in range(3))
         for head in range(heads):
-            rad_f, rad_r = radii_ref[head, 0], radii_ref[head, 1]
+            rad_f, rad_r = radii_ref[0, head], radii_ref[1, head]
             both += rad_f * rad_r
             side += rad_f * (1 - rad_r)
             edge += (1 - rad_f) * rad_r
         starts = [both + side, heads - edge, both, 0]
         for head in range(heads):
-            rad_f, rad_r = radii_ref[head, 0], radii_ref[head, 1]
+            rad_f, rad_r = radii_ref[0, head], radii_ref[1, head]
             kind = 2 * rad_f + rad_r
             place = sum(jnp.where(kind == i, starts[i], 0) for i in range(4))
             slot = place + jnp.where(kind == 1, both - (heads - edge), jnp.where(kind == 3, 0, edge))
@@ -39,7 +39,7 @@
             meta_ref[0, place] = head
             meta_ref[1, place] = rad_f
             meta_ref[2, place] = rad_r
-            meta_ref[3, place] = radii_ref[head, 2]
+            meta_ref[3, place] = radii_ref[2, head]
             meta_ref[4, place] = slot
             meta_ref[5, place] = head // (heads // 2)
             meta_ref[6, place] = head % (heads // 2)
@@ -73,52 +73,85 @@
 
 def pack_heads(order, sources, groups, tile, tiles, slots=None, edge_groups=()):
     tokens, width = sources[0].shape
+    kinds = len(sources)
     scalars = [order] if slots is None else [order, slots]
-    edge_shapes = [(count, len(sources), tile, HEAD_DIM) for _, count in edge_groups]
+    shapes = [(count, len(which), tokens, HEAD_DIM) for _, count, which in groups]
+    whole = len(shapes)
+    shapes += [(count, kinds, tile, HEAD_DIM) for _, count in edge_groups for _ in range(2)]
 
     def kernel(*refs):
-        order_ref, refs = refs[0], refs[len(scalars) - 1 :]
-        slot_ref, refs = refs[0], refs[1:]
-        ins, outs = refs[: len(sources)], refs[len(sources) :]
-
-        def gather(from_ref, first, count, which, out):
-            def copy(at, carry):
-                columns = pl.ds(pl.multiple_of(from_ref[first + at] * HEAD_DIM, HEAD_DIM), HEAD_DIM)
+        scalar_refs, refs = refs[: len(scalars)], refs[len(scalars) :]
+        ins, refs = refs[:kinds], refs[kinds:]
+        outs, refs = refs[: len(shapes)], refs[len(shapes) :]
+        in_buf, out_bufs, (in_sem, out_sem) = refs[0], refs[1 : 1 + len(shapes)], refs[1 + len(shapes) :]
+
+        def tile_rows(at):
+            return pl.ds(pl.multiple_of(at * tile, tile), tile)
+
+        def in_copies(at):
+            return [
+                pltpu.make_async_copy(x.at[tile_rows(at)], in_buf.at[i, tile_rows(at)], in_sem.at[i, at])
+                for i, x in enumerate(ins)
+            ]
+
+        def out_copies(at):
+            return [
+                pltpu.make_async_copy(
+                    out_bufs[i].at[:, :, tile_rows(at)], outs[i].at[:, :, tile_rows(at)], out_sem.at[i, at]
+                )
+                for i in range(whole)
+            ]
+
+        def edge_copy(i):
+            return pltpu.make_async_copy(out_bufs[i], outs[i], out_sem.at[i, 0])
+
+        def gather(from_ref, first, count, which, out, at, to):
+            def copy(head, carry):
+                columns = pl.ds(pl.multiple_of(from_ref[first + head] * HEAD_DIM, HEAD_DIM), HEAD_DIM)
                 for index, source in enumerate(which):
-                    out[at, index] = ins[source][:, columns]
+                    out[head, index, to, :] = in_buf[source, tile_rows(at), columns]
                 return carry
 
             lax.fori_loop(0, count, copy, 0, unroll=2)
 
-        for (first, count, which), out in zip(groups, outs):
-            gather(order_ref, first, count, which, out)
-        if slots is not None:
-            for i, at in enumerate((0, tiles - 1)):
-
-                @pl.when(pl.program_id(0) == at)
-                def _():
-                    for j, (first, count) in enumerate(edge_groups):
-                        gather(slot_ref, first, count, range(len(sources)), outs[len(groups) + 2 * j + i])
-
-    in_spec = pl.BlockSpec((tile, width), lambda step, *refs: (step, 0))
-    out_specs = [
-        pl.BlockSpec((count, len(which), tile, HEAD_DIM), lambda step, *refs: (0, 0, step, 0))
-        for _, count, which in groups
-    ]
-    shapes = [(count, len(which), tokens, HEAD_DIM) for _, count, which in groups]
-    if slots is not None:
-        for shape in edge_shapes:
-            out_specs += [pl.BlockSpec(shape, lambda step, *refs: (0, 0, 0, 0))] * 2
-            shapes += [shape] * 2
+        def each(at, carry):
+            for copy in in_copies(at):
+                copy.wait()
+            for (first, count, which), out in zip(groups, out_bufs):
+                gather(scalar_refs[0], first, count, which, out, at, tile_rows(at))
+            for copy in out_copies(at):
+                copy.start()
+            for j, (first, count) in enumerate(edge_groups):
+                for i, end in enumerate((0, tiles - 1)):
+
+                    @pl.when(at == end)
+                    def _():
+                        place = whole + 2 * j + i
+                        gather(scalar_refs[1], first, count, range(kinds), out_bufs[place], at, pl.ds(0, tile))
+                        edge_copy(place).start()
+
+            return carry
+
+        for at in range(tiles):
+            for copy in in_copies(at):
+                copy.start()
+        lax.fori_loop(0, tiles, each, 0)
+        for at in range(tiles):
+            for copy in out_copies(at):
+                copy.wait()
+        for i in range(whole, len(shapes)):
+            edge_copy(i).wait()
+
+    smem, anywhere = pl.BlockSpec(memory_space=pltpu.SMEM), pl.BlockSpec(memory_space=pl.ANY)
+    dtype = sources[0].dtype
     return pl.pallas_call(
         kernel,
-        out_shape=[jax.ShapeDtypeStruct(shape, sources[0].dtype) for shape in shapes],
-        grid_spec=pltpu.PrefetchScalarGridSpec(
-            num_scalar_prefetch=len(scalars),
-            grid=(tiles,),
-            in_specs=[in_spec] * len(sources),
-            out_specs=out_specs,
-        ),
+        out_shape=[jax.ShapeDtypeStruct(shape, dtype) for shape in shapes],
+        in_specs=[smem] * len(scalars) + [anywhere] * kinds,
+        out_specs=[anywhere] * len(shapes),
+        scratch_shapes=[pltpu.VMEM((kinds, tokens, width), dtype)]
+        + [pltpu.VMEM(shape, dtype) for shape in shapes]
+        + [pltpu.SemaphoreType.DMA((kinds, tiles)), pltpu.SemaphoreType.DMA((len(shapes), tiles))],
         compiler_params=pltpu.CompilerParams(vmem_limit_bytes=VMEM_BYTES),
     )(*scalars, *sources)
 
@@ -411,7 +444,7 @@
     up = [(i + 1, i) for i in range(height_total - 1)]
     levels = [(heads, heads, heads), (16, 10, 16), (13, 8, 14), (10, 6, 12)]
 
-    meta, slots, flags, level = plan_heads(window_radii, frame_valid, levels)
+    meta, slots, flags, level = plan_heads(window_radii.T, frame_valid, levels)
     order = meta[0]
 
     col = np.arange(tile) % col_total // COL_TILE

time: 128 us -> 146 us (1.14)
  the two profiles are of different devices: /device:TPU:54 before, /device:TPU:95 now
where the time goes in v2:
time: 146 us; the launch traced here: 144 us
  waiting for transfers between devices  58.9 us (40%)
  Pallas kernels  57.5 us (39%)
  starting transfers between devices  22.1 us (15%)
  local copies, waits for them, and re-layouts  3.91 us (3%)
    pallas_call x4, Pallas kernels, chunk(): pl.pallas_call(kernel, out_shape=jax.ShapeDtypeStruct(shape, out_type), i...  47 us
    ppermute x2, waiting for transfers between devices, call(): beyond = [lax.ppermute(x, GRID_AXES, outer_pairs) for x in packed]  45.6 us
    pallas_call x2, Pallas kernels, pack_heads(): pl.pallas_call(kernel, out_shape=[jax.ShapeDtypeStruct(shape, dtype) for...  8.73 us
    ppermute x2, waiting for transfers between devices, trade_edges(): return (lax.ppermute(high, 'height', down), lax.ppermute(low, 'height', up))  7.65 us
    ppermute x2, starting transfers between devices, call(): beyond = [lax.ppermute(x, GRID_AXES, outer_pairs) for x in packed]  7.56 us
    ppermute x2, starting transfers between devices, trade_edges(): return (lax.ppermute(high, 'height', down), lax.ppermute(low, 'height', up))  6.19 us
    ppermute x1, starting transfers between devices, trade_corners(): lax.ppermute(beyond[:, :, :tile], 'height', up)  4.81 us
  transfers between devices with their start and end apart: 11, of which 6 were waited for; matrix products, arithmetic and copies ran while one was open for 2% of the time, Pallas kernels for 26%

profile of v2, /device:TPU:95, one launch (start us, length us, event | category | flops | bytes accessed | tf_op | source)
XLA Modules:
  0.0 144.0 jit_solution(17600430632598266984)
XLA Ops:
  0.0 1.7 %shard_map.77 = (s32[8,20]{1,0:T(8,128)S(1)}, s32[20]{0:T(128)S(1)}, s32[8]{0:T(128)S(1)}, s32[1]{0:T(128)}) custom-call(s32[3,20]{1,0:T(4,128)} %bitcast.27, s32[16]{0:T(128)} %valid_ref.1), custom_call_target="tpu_custom_call" | custom-call | tf_op jit(solution)/shard_map/pallas_call | solution.py:66
  2.4 141.4 %conditional.1 = (bf16[1,8,48,5120]{3,2,1,0:T(8,128)(2,1)}) conditional(s32[]{:T(128)} %bitcast.5, (s32[20]{0:T(128)S(1)}, s32[20]{0:T(128)S(1)}, bf16[384,2560]{1,0:T(8,128)(2,1)}, bf16[384,2560]{1,0:T(8,128)(2,1)}, bf16[384,2560]{1,0:T(8,128)(2,1)}, /*index=5*/s32[8,20]{1,0:T(8,128)S(1)}, s32[8]{0:T(128)S(1)}, ...), branch_computations={%region_0.0_spmd, %region_1.0_spmd, %region_2.0_spmd, %region_3.0_... | conditional | bytes 129401536 | solution.py:507
  2.4 0.8 collective-permute-start.23
  3.2 0.0 copy-start.1
  3.2 4.4 %branch_1_fun.6 = (bf16[10,2,384,128]{3,2,1,0:T(8,128)(2,1)}, bf16[6,2,384,128]{3,2,1,0:T(8,128)(2,1)}, bf16[16,2,96,128]{3,2,1,0:T(8,128)(2,1)}, bf16[16,2,96,128]{3,2,1,0:T(8,128)(2,1)}) custom-call(s32[20]{0:T(128)S(1)} %get-tuple-element.113.refs_0_, s32[20]{0:T(128)S(1)} %get-tuple-element.114.refs_1_, bf16[384,2560]{1,0:T(8,128)(2,1)} %get-tuple-element.115.refs_2_, ...), custom_call_target="tpu_custom_call" | custom-call | tf_op jit(solution)/shard_map/cond/branch_1_fun/pallas_call | solution.py:147
  7.6 1.3 collective-permute-start.13
  8.9 4.9 %collective-permute-start.14 = (bf16[16,2,96,128]{3,2,1,0:T(8,128)(2,1)}, bf16[16,2,96,128]{3,2,1,0:T(8,128)(2,1)}, u32[]{:S(2)}, u32[]{:S(2)}) collective-permute-start(bf16[16,2,96,128]{3,2,1,0:T(8,128)(2,1)} %get-tuple-element.118), channel_id=1, source_target_pairs={{2,0},{4,2},{6,4},{8,6},{10,8},{12,10},{14,12},{3,1},{5,3},{7,5},{... | collective-permute-start | bytes 2359304 | tf_op jit(solution)/shard_map/cond/branch_1_fun/ppermute | solution.py:455
  13.8 3.9 %collective-permute-start.20 = (bf16[10,2,384,128]{3,2,1,0:T(8,128)(2,1)}, bf16[10,2,384,128]{3,2,1,0:T(8,128)(2,1)}, u32[]{:S(2)}, u32[]{:S(2)}) collective-permute-start(bf16[10,2,384,128]{3,2,1,0:T(8,128)(2,1)} %get-tuple-element.133.refs_1_), channel_id=1, source_target_pairs={{1,16},{17,32},{33,48},{49,64},{65,80},{81,96},{97,112},{16,1},{32... | collective-permute-start | bytes 5898248 | tf_op jit(solution)/shard_map/cond/branch_1_fun/ppermute | solution.py:474
  17.6 0.1 collective-permute-start.19
  17.7 0.0 copy-done.1
  17.8 4.4 %branch_1_fun.7 = (bf16[10,1,384,128]{3,2,1,0:T(8,128)(2,1)}, bf16[6,1,384,128]{3,2,1,0:T(8,128)(2,1)}, bf16[4,1,384,128]{3,2,1,0:T(8,128)(2,1)}, bf16[4,2,384,128]{3,2,1,0:T(8,128)(2,1)}) custom-call(s32[20]{0:T(128)S(1)} %get-tuple-element.113.refs_0_, bf16[384,2560]{1,0:T(8,128)(2,1)} %get-tuple-element.119.refs_1_, bf16[384,2560]{1,0:T(8,128)(2,1)S(1)} %copy-done.1, ...), custom_call_target="tpu_custom_call" | custom-call | tf_op jit(solution)/shard_map/cond/branch_1_fun/pallas_call | solution.py:147
  22.1 6.8 %collective-permute-done.13.refs_2_.refs_6_ = bf16[16,2,96,128]{3,2,1,0:T(8,128)(2,1)} collective-permute-done((bf16[16,2,96,128]{3,2,1,0:T(8,128)(2,1)}, bf16[16,2,96,128]{3,2,1,0:T(8,128)(2,1)}, u32[]{:S(2)}, u32[]{:S(2)}) %collective-permute-start.13) | collective-permute-done | bytes 786464 | tf_op jit(solution)/shard_map/cond/branch_1_fun/ppermute | solution.py:455
  28.9 0.9 collective-permute-done.14.refs_3_.refs_7_
  29.8 1.1 collective-permute-start.15
  30.9 0.0 collective-permute-start.16
  30.9 2.1 %collective-permute-done.15.refs_8_ = bf16[16,2,96,128]{3,2,1,0:T(8,128)(2,1)S(1)} collective-permute-done((bf16[16,2,96,128]{3,2,1,0:T(8,128)(2,1)}, bf16[16,2,96,128]{3,2,1,0:T(8,128)(2,1)S(1)}, u32[]{:S(2)}, u32[]{:S(2)}) %collective-permute-start.15) | collective-permute-done | bytes 786464 | tf_op jit(solution)/shard_map/cond/branch_1_fun/ppermute | solution.py:458
  33.0 0.0 copy-start.12
  33.0 3.7 %collective-permute-start.18 = (bf16[6,2,384,128]{3,2,1,0:T(8,128)(2,1)}, bf16[6,2,384,128]{3,2,1,0:T(8,128)(2,1)S(1)}, u32[]{:S(2)}, u32[]{:S(2)}) collective-permute-start(bf16[6,2,384,128]{3,2,1,0:T(8,128)(2,1)} %get-tuple-element.131.refs_1_), channel_id=1, source_target_pairs={{1,16},{17,32},{33,48},{49,64},{65,80},{81,96},{97,112},{16,1},{32... | collective-permute-start | bytes 3538952 | tf_op jit(solution)/shard_map/cond/branch_1_fun/ppermute | solution.py:474
  36.7 0.0 collective-permute-done.16.refs_9_
  36.7 0.0 copy-start.13
  36.7 0.3 collective-permute-start.17
  37.0 0.0 copy-done.12
  37.0 0.6 copy-done.13
  37.6 0.0 copy-start.5
  37.6 5.4 %branch_1_fun.8.refs_0_ = bf16[4,384,128]{2,1,0:T(8,128)(2,1)} custom-call(s32[8,20]{1,0:T(8,128)S(1)} %get-tuple-element.110.meta_ref, s32[8]{0:T(128)S(1)} %get-tuple-element.111.flag_ref, f32[2,96,96]{2,1,0:T(8,128)} %get-tuple-element.112.mask_ref, bf16[4,1,384,128]{3,2,1,0:T(8,128)(2,1)} %get-tuple-element.134.refs_0_, ...), custom_call_target="tpu_custom_call" | custom-call | tf_op jit(solution)/shard_map/cond/branch_1_fun/pallas_call | solution.py:422
  43.1 45.6 %collective-permute-done.20.refs_3_ = bf16[10,2,384,128]{3,2,1,0:T(8,128)(2,1)} collective-permute-done((bf16[10,2,384,128]{3,2,1,0:T(8,128)(2,1)}, bf16[10,2,384,128]{3,2,1,0:T(8,128)(2,1)}, u32[]{:S(2)}, u32[]{:S(2)}) %collective-permute-start.20) | collective-permute-done | bytes 1966112 | tf_op jit(solution)/shard_map/cond/branch_1_fun/ppermute | solution.py:474
  88.7 2.3 %fusion.2 = (bf16[10,2,96,128]{3,2,1,0:T(8,128)(2,1)}, bf16[10,2,96,128]{3,2,1,0:T(8,128)(2,1)}) fusion(bf16[10,2,384,128]{3,2,1,0:T(8,128)(2,1)} %collective-permute-done.20.refs_3_), kind=kLoop, calls=%fused_computation.3 | loop fusion | bytes 1966080 | tf_op jit(solution)/shard_map/cond/branch_1_fun/slice | solution.py:463
  90.9 1.3 collective-permute-start.21
  92.2 0.0 collective-permute-done.23.refs_2_.refs_6_
  92.2 4.8 %collective-permute-start.22 = (bf16[10,2,96,128]{3,2,1,0:T(8,128)(2,1)}, bf16[10,2,96,128]{3,2,1,0:T(8,128)(2,1)}, u32[]{:S(2)}, u32[]{:S(2)}) collective-permute-start(bf16[10,2,96,128]{3,2,1,0:T(8,128)(2,1)} %get-tuple-element.237), channel_id=1, source_target_pairs={{2,0},{4,2},{6,4},{8,6},{10,8},{12,10},{14,12},{3,1},{5,3},{7,5},{... | collective-permute-start | bytes 1474568 | tf_op jit(solution)/shard_map/cond/branch_1_fun/ppermute | solution.py:463
  97.0 0.0 copy-done.5
  97.0 6.6 %branch_1_fun.9.refs_7_ = f32[384,5120]{1,0:T(8,128)} custom-call(s32[8,20]{1,0:T(8,128)S(1)} %get-tuple-element.110.meta_ref, s32[8]{0:T(128)S(1)} %get-tuple-element.111.flag_ref, f32[2,96,96]{2,1,0:T(8,128)S(1)} %copy-done.5, bf16[4,384,128]{2,1,0:T(8,128)(2,1)} %branch_1_fun.8.refs_0_, bf16[1280,5120]{1,0:T(8,128)(2,1)} %get-tuple-element.140.refs_1_.refs_5_, ...), custom_call_target="tpu_custom_call" | custom-call | tf_op jit(solution)/shard_map/cond/branch_1_fun/pallas_call | solution.py:422
  103.7 2.5 %collective-permute-done.21.refs_4_ = bf16[10,2,96,128]{3,2,1,0:T(8,128)(2,1)S(1)} collective-permute-done((bf16[10,2,96,128]{3,2,1,0:T(8,128)(2,1)}, bf16[10,2,96,128]{3,2,1,0:T(8,128)(2,1)S(1)}, u32[]{:S(2)}, u32[]{:S(2)}) %collective-permute-start.21) | collective-permute-done | bytes 491552 | tf_op jit(solution)/shard_map/cond/branch_1_fun/ppermute | solution.py:462
  106.1 0.0 copy-start.18
  106.1 1.1 collective-permute-done.22.refs_5_
  107.2 0.0 collective-permute-done.19.refs_2_
  107.2 0.0 copy-done.18
  107.2 16.3 %branch_1_fun.10.refs_4_ = bf16[10,384,128]{2,1,0:T(8,128)(2,1)} custom-call(s32[8,20]{1,0:T(8,128)S(1)} %get-tuple-element.110.meta_ref, s32[8]{0:T(128)S(1)} %get-tuple-element.111.flag_ref, f32[2,96,96]{2,1,0:T(8,128)S(1)} %copy-done.5, bf16[10,1,384,128]{3,2,1,0:T(8,128)(2,1)} %get-tuple-element.132.refs_0_, ...), custom_call_target="tpu_custom_call" | custom-call | tf_op jit(solution)/shard_map/cond/branch_1_fun/pallas_call | solution.py:422
  123.6 0.0 collective-permute-done.18.refs_3_
  123.6 0.0 copy-start.11
  123.6 0.0 collective-permute-done.17.refs_2_
  123.6 1.0 copy-done.11
  124.6 18.6 %branch_1_fun.11 = bf16[384,5120]{1,0:T(8,128)(2,1)} custom-call(s32[8,20]{1,0:T(8,128)S(1)} %get-tuple-element.110.meta_ref, s32[8]{0:T(128)S(1)} %get-tuple-element.111.flag_ref, f32[2,96,96]{2,1,0:T(8,128)S(1)} %copy-done.5, bf16[6,1,384,128]{3,2,1,0:T(8,128)(2,1)} %get-tuple-element.130.refs_0_, bf16[6,2,384,128]{3,2,1,0:T(8,128)(2,1)} %get-tuple-element.131.refs_1_, ...), custom_call_target="tpu_custom_call" | custom-call | tf_op jit(solution)/shard_map/cond/branch_1_fun/pallas_call | solution.py:422
  (1 shorter events, 0.0 us)
Async XLA Ops:
  2.4 89.8 %collective-permute-start.23 = (bf16[1280,5120]{1,0:T(8,128)(2,1)}, bf16[1280,5120]{1,0:T(8,128)(2,1)}, u32[]{:S(2)}, u32[]{:S(2)}) collective-permute-start(bf16[1280,5120]{1,0:T(8,128)(2,1)} %get-tuple-element.140.refs_1_.refs_5_), channel_id=1, source_target_pairs={{0,1},{1,0},{2,3},{3,2},{4,5},{5,4},{6,7},{7,6},{8,9},{9,8},{10,11... | collective-permute-start | bytes 39321608 | tf_op jit(solution)/shard_map/cond/branch_1_fun/ppermute | solution.py:476
  3.2 14.6 %copy-start.1 = (bf16[384,2560]{1,0:T(8,128)(2,1)S(1)}, bf16[384,2560]{1,0:T(8,128)(2,1)}, u32[]{:S(2)}) copy-start(bf16[384,2560]{1,0:T(8,128)(2,1)} %get-tuple-element.115.refs_2_) | copy-start | bytes 5898244 | tf_op jit(solution)/shard_map/cond
  7.6 21.4 %collective-permute-start.13 = (bf16[16,2,96,128]{3,2,1,0:T(8,128)(2,1)}, bf16[16,2,96,128]{3,2,1,0:T(8,128)(2,1)}, u32[]{:S(2)}, u32[]{:S(2)}) collective-permute-start(bf16[16,2,96,128]{3,2,1,0:T(8,128)(2,1)} %get-tuple-element.117), channel_id=1, source_target_pairs={{0,2},{2,4},{4,6},{6,8},{8,10},{10,12},{12,14},{1,3},{3,5},{5,7},{... | collective-permute-start | bytes 2359304 | tf_op jit(solution)/shard_map/cond/branch_1_fun/ppermute | solution.py:455
  8.9 20.9 %collective-permute-start.14 = (bf16[16,2,96,128]{3,2,1,0:T(8,128)(2,1)}, bf16[16,2,96,128]{3,2,1,0:T(8,128)(2,1)}, u32[]{:S(2)}, u32[]{:S(2)}) collective-permute-start(bf16[16,2,96,128]{3,2,1,0:T(8,128)(2,1)} %get-tuple-element.118), channel_id=1, source_target_pairs={{2,0},{4,2},{6,4},{8,6},{10,8},{12,10},{14,12},{3,1},{5,3},{7,5},{... | collective-permute-start | bytes 2359304 | tf_op jit(solution)/shard_map/cond/branch_1_fun/ppermute | solution.py:455
  13.8 74.9 %collective-permute-start.20 = (bf16[10,2,384,128]{3,2,1,0:T(8,128)(2,1)}, bf16[10,2,384,128]{3,2,1,0:T(8,128)(2,1)}, u32[]{:S(2)}, u32[]{:S(2)}) collective-permute-start(bf16[10,2,384,128]{3,2,1,0:T(8,128)(2,1)} %get-tuple-element.133.refs_1_), channel_id=1, source_target_pairs={{1,16},{17,32},{33,48},{49,64},{65,80},{81,96},{97,112},{16,1},{32... | collective-permute-start | bytes 5898248 | tf_op jit(solution)/shard_map/cond/branch_1_fun/ppermute | solution.py:474
  17.6 89.6 %collective-permute-start.19 = (bf16[10,2,384,128]{3,2,1,0:T(8,128)(2,1)}, bf16[10,2,384,128]{3,2,1,0:T(8,128)(2,1)}, u32[]{:S(2)}, u32[]{:S(2)}) collective-permute-start(bf16[10,2,384,128]{3,2,1,0:T(8,128)(2,1)} %get-tuple-element.133.refs_1_), channel_id=1, source_target_pairs={{0,1},{1,0},{2,3},{3,2},{4,5},{5,4},{6,7},{7,6},{8,9},{9,8},{10,11... | collective-permute-start | bytes 5898248 | tf_op jit(solution)/shard_map/cond/branch_1_fun/ppermute | solution.py:475
  29.8 3.2 %collective-permute-start.15 = (bf16[16,2,96,128]{3,2,1,0:T(8,128)(2,1)}, bf16[16,2,96,128]{3,2,1,0:T(8,128)(2,1)S(1)}, u32[]{:S(2)}, u32[]{:S(2)}) collective-permute-start(bf16[16,2,96,128]{3,2,1,0:T(8,128)(2,1)} %collective-permute-done.13.refs_2_.refs_6_), channel_id=1, source_target_pairs={{0,1},{1,0},{2,3},{3,2},{4,5},{5,4},{6,7},{7,6},{8,9},{9,8},{10,11... | collective-permute-start | bytes 2359304 | tf_op jit(solution)/shard_map/cond/branch_1_fun/ppermute | solution.py:458
  30.9 5.8 %collective-permute-start.16 = (bf16[16,2,96,128]{3,2,1,0:T(8,128)(2,1)}, bf16[16,2,96,128]{3,2,1,0:T(8,128)(2,1)S(1)}, u32[]{:S(2)}, u32[]{:S(2)}) collective-permute-start(bf16[16,2,96,128]{3,2,1,0:T(8,128)(2,1)} %collective-permute-done.14.refs_3_.refs_7_), channel_id=1, source_target_pairs={{0,1},{1,0},{2,3},{3,2},{4,5},{5,4},{6,7},{7,6},{8,9},{9,8},{10,11... | collective-permute-start | bytes 2359304 | tf_op jit(solution)/shard_map/cond/branch_1_fun/ppermute | solution.py:458
  33.0 4.0 %copy-start.12 = (bf16[16,2,96,128]{3,2,1,0:T(8,128)(2,1)}, bf16[16,2,96,128]{3,2,1,0:T(8,128)(2,1)S(1)}, u32[]{:S(2)}) copy-start(bf16[16,2,96,128]{3,2,1,0:T(8,128)(2,1)S(1)} %collective-permute-done.15.refs_8_) | copy-start | bytes 2359300 | tf_op jit(solution)/shard_map/cond
  33.0 90.6 %collective-permute-start.18 = (bf16[6,2,384,128]{3,2,1,0:T(8,128)(2,1)}, bf16[6,2,384,128]{3,2,1,0:T(8,128)(2,1)S(1)}, u32[]{:S(2)}, u32[]{:S(2)}) collective-permute-start(bf16[6,2,384,128]{3,2,1,0:T(8,128)(2,1)} %get-tuple-element.131.refs_1_), channel_id=1, source_target_pairs={{1,16},{17,32},{33,48},{49,64},{65,80},{81,96},{97,112},{16,1},{32... | collective-permute-start | bytes 3538952 | tf_op jit(solution)/shard_map/cond/branch_1_fun/ppermute | solution.py:474
  36.7 0.9 copy-start.13
  36.7 86.9 %collective-permute-start.17 = (bf16[6,2,384,128]{3,2,1,0:T(8,128)(2,1)}, bf16[6,2,384,128]{3,2,1,0:T(8,128)(2,1)}, u32[]{:S(2)}, u32[]{:S(2)}) collective-permute-start(bf16[6,2,384,128]{3,2,1,0:T(8,128)(2,1)} %get-tuple-element.131.refs_1_), channel_id=1, source_target_pairs={{0,1},{1,0},{2,3},{3,2},{4,5},{5,4},{6,7},{7,6},{8,9},{9,8},{10,11... | collective-permute-start | bytes 3538952 | tf_op jit(solution)/shard_map/cond/branch_1_fun/ppermute | solution.py:475
  37.6 59.4 %copy-start.5 = (f32[2,96,96]{2,1,0:T(8,128)S(1)}, f32[2,96,96]{2,1,0:T(8,128)}, u32[]{:S(2)}) copy-start(f32[2,96,96]{2,1,0:T(8,128)} %get-tuple-element.112.mask_ref) | copy-start | bytes 221188 | tf_op jit(solution)/shard_map/cond
  90.9 15.2 %collective-permute-start.21 = (bf16[10,2,96,128]{3,2,1,0:T(8,128)(2,1)}, bf16[10,2,96,128]{3,2,1,0:T(8,128)(2,1)S(1)}, u32[]{:S(2)}, u32[]{:S(2)}) collective-permute-start(bf16[10,2,96,128]{3,2,1,0:T(8,128)(2,1)} %get-tuple-element.238), channel_id=1, source_target_pairs={{0,2},{2,4},{4,6},{6,8},{8,10},{10,12},{12,14},{1,3},{3,5},{5,7},{... | collective-permute-start | bytes 1474568 | tf_op jit(solution)/shard_map/cond/branch_1_fun/ppermute | solution.py:462
  92.2 15.0 %collective-permute-start.22 = (bf16[10,2,96,128]{3,2,1,0:T(8,128)(2,1)}, bf16[10,2,96,128]{3,2,1,0:T(8,128)(2,1)}, u32[]{:S(2)}, u32[]{:S(2)}) collective-permute-start(bf16[10,2,96,128]{3,2,1,0:T(8,128)(2,1)} %get-tuple-element.237), channel_id=1, source_target_pairs={{2,0},{4,2},{6,4},{8,6},{10,8},{12,10},{14,12},{3,1},{5,3},{7,5},{... | collective-permute-start | bytes 1474568 | tf_op jit(solution)/shard_map/cond/branch_1_fun/ppermute | solution.py:463
  106.1 1.1 copy-start.18
  123.6 1.0 copy-start.11

commit v3 on v2

--- a/solution.py
+++ b/solution.py
@@ -442,7 +442,7 @@
     swap = [(0, 1), (1, 0)]
     down = [(i, i + 1) for i in range(height_total - 1)]
     up = [(i + 1, i) for i in range(height_total - 1)]
-    levels = [(heads, heads, heads), (16, 10, 16), (13, 8, 14), (10, 6, 12)]
+    levels = [(heads, heads, heads), (14, 10, 14), (11, 8, 15), (9, 6, 13)]
 
     meta, slots, flags, level = plan_heads(window_radii.T, frame_valid, levels)
     order = meta[0]

time: 146 us -> 115 us (0.79)
  the two profiles are of different devices: /device:TPU:95 before, /device:TPU:11 now
where the time goes in v3:
time: 115 us; the launch traced here: 114 us
  Pallas kernels  55.6 us (48%)
  starting transfers between devices  39.8 us (35%)
  waiting for transfers between devices  14.8 us (13%)
  local copies, waits for them, and re-layouts  2.05 us (2%)
    pallas_call x4, Pallas kernels, chunk(): pl.pallas_call(kernel, out_shape=jax.ShapeDtypeStruct(shape, out_type), i...  45.4 us
    ppermute x1, starting transfers between devices, trade_corners(): lax.ppermute(beyond[:, :, :tile], 'height', up)  21.2 us
    ppermute x2, waiting for transfers between devices, trade_edges(): return (lax.ppermute(high, 'height', down), lax.ppermute(low, 'height', up))  12.9 us
    pallas_call x2, Pallas kernels, pack_heads(): pl.pallas_call(kernel, out_shape=[jax.ShapeDtypeStruct(shape, dtype) for...  8.52 us
    ppermute x2, starting transfers between devices, call(): beyond = [lax.ppermute(x, GRID_AXES, outer_pairs) for x in packed]  7.04 us
    ppermute x2, starting transfers between devices, trade_edges(): return (lax.ppermute(high, 'height', down), lax.ppermute(low, 'height', up))  6.15 us
    ppermute x1, starting transfers between devices, trade_corners(): lax.ppermute(beyond[:, :, tokens - tile:], 'height', down)  3.91 us
  transfers between devices with their start and end apart: 11, of which 3 were waited for; matrix products, arithmetic and copies ran while one was open for 1% of the time, Pallas kernels for 35%

profile of v3, /device:TPU:11, one launch (start us, length us, event | category | flops | bytes accessed | tf_op | source)
XLA Modules:
  0.0 114.0 jit_solution(2933579645481750693)
XLA Ops:
  0.0 1.7 %shard_map.77 = (s32[8,20]{1,0:T(8,128)S(1)}, s32[20]{0:T(128)S(1)}, s32[8]{0:T(128)S(1)}, s32[1]{0:T(128)}) custom-call(s32[3,20]{1,0:T(4,128)} %bitcast.27, s32[16]{0:T(128)} %valid_ref.1), custom_call_target="tpu_custom_call" | custom-call | tf_op jit(solution)/shard_map/pallas_call | solution.py:66
  2.4 111.3 %conditional.1 = (bf16[1,8,48,5120]{3,2,1,0:T(8,128)(2,1)}) conditional(s32[]{:T(128)} %bitcast.5, (s32[20]{0:T(128)S(1)}, s32[20]{0:T(128)S(1)}, bf16[384,2560]{1,0:T(8,128)(2,1)}, bf16[384,2560]{1,0:T(8,128)(2,1)}, bf16[384,2560]{1,0:T(8,128)(2,1)}, /*index=5*/s32[8,20]{1,0:T(8,128)S(1)}, s32[8]{0:T(128)S(1)}, ...), branch_computations={%region_0.0_spmd, %region_1.0_spmd, %region_2.0_spmd, %region_3.0_... | conditional | bytes 129401536 | solution.py:507
  2.7 0.8 collective-permute-start.34
  3.4 0.0 copy-start.2
  3.4 4.1 %branch_2_fun.6 = (bf16[8,2,384,128]{3,2,1,0:T(8,128)(2,1)}, bf16[3,2,384,128]{3,2,1,0:T(8,128)(2,1)}, bf16[15,2,96,128]{3,2,1,0:T(8,128)(2,1)}, bf16[15,2,96,128]{3,2,1,0:T(8,128)(2,1)}) custom-call(s32[20]{0:T(128)S(1)} %get-tuple-element.151.refs_0_, s32[20]{0:T(128)S(1)} %get-tuple-element.152.refs_1_, bf16[384,2560]{1,0:T(8,128)(2,1)} %get-tuple-element.153.refs_2_, ...), custom_call_target="tpu_custom_call" | custom-call | tf_op jit(solution)/shard_map/cond/branch_2_fun/pallas_call | solution.py:147
  7.5 3.3 %collective-permute-start.31 = (bf16[8,2,384,128]{3,2,1,0:T(8,128)(2,1)}, bf16[8,2,384,128]{3,2,1,0:T(8,128)(2,1)}, u32[]{:S(2)}, u32[]{:S(2)}) collective-permute-start(bf16[8,2,384,128]{3,2,1,0:T(8,128)(2,1)} %get-tuple-element.171.refs_1_), channel_id=1, source_target_pairs={{1,16},{17,32},{33,48},{49,64},{65,80},{81,96},{97,112},{16,1},{32... | collective-permute-start | bytes 4718600 | tf_op jit(solution)/shard_map/cond/branch_2_fun/ppermute | solution.py:474
  10.8 3.1 %collective-permute-start.24 = (bf16[15,2,96,128]{3,2,1,0:T(8,128)(2,1)}, bf16[15,2,96,128]{3,2,1,0:T(8,128)(2,1)}, u32[]{:S(2)}, u32[]{:S(2)}) collective-permute-start(bf16[15,2,96,128]{3,2,1,0:T(8,128)(2,1)} %get-tuple-element.155), channel_id=1, source_target_pairs={{0,2},{2,4},{4,6},{6,8},{8,10},{10,12},{12,14},{1,3},{3,5},{5,7},{... | collective-permute-start | bytes 2211848 | tf_op jit(solution)/shard_map/cond/branch_2_fun/ppermute | solution.py:455
  14.0 3.0 %collective-permute-start.25 = (bf16[15,2,96,128]{3,2,1,0:T(8,128)(2,1)}, bf16[15,2,96,128]{3,2,1,0:T(8,128)(2,1)}, u32[]{:S(2)}, u32[]{:S(2)}) collective-permute-start(bf16[15,2,96,128]{3,2,1,0:T(8,128)(2,1)} %get-tuple-element.156), channel_id=1, source_target_pairs={{2,0},{4,2},{6,4},{8,6},{10,8},{12,10},{14,12},{3,1},{5,3},{7,5},{... | collective-permute-start | bytes 2211848 | tf_op jit(solution)/shard_map/cond/branch_2_fun/ppermute | solution.py:455
  17.0 0.1 collective-permute-start.30
  17.1 0.0 copy-done.2
  17.1 4.4 %branch_2_fun.7 = (bf16[8,1,384,128]{3,2,1,0:T(8,128)(2,1)}, bf16[3,1,384,128]{3,2,1,0:T(8,128)(2,1)}, bf16[9,1,384,128]{3,2,1,0:T(8,128)(2,1)}, bf16[9,2,384,128]{3,2,1,0:T(8,128)(2,1)}) custom-call(s32[20]{0:T(128)S(1)} %get-tuple-element.151.refs_0_, bf16[384,2560]{1,0:T(8,128)(2,1)} %get-tuple-element.157.refs_1_, bf16[384,2560]{1,0:T(8,128)(2,1)S(1)} %copy-done.2, ...), custom_call_target="tpu_custom_call" | custom-call | tf_op jit(solution)/shard_map/cond/branch_2_fun/pallas_call | solution.py:147
  21.6 9.6 %collective-permute-done.24.refs_2_.refs_6_ = bf16[15,2,96,128]{3,2,1,0:T(8,128)(2,1)} collective-permute-done((bf16[15,2,96,128]{3,2,1,0:T(8,128)(2,1)}, bf16[15,2,96,128]{3,2,1,0:T(8,128)(2,1)}, u32[]{:S(2)}, u32[]{:S(2)}) %collective-permute-start.24) | collective-permute-done | bytes 737312 | tf_op jit(solution)/shard_map/cond/branch_2_fun/ppermute | solution.py:455
  31.2 3.3 %collective-permute-done.25.refs_3_.refs_7_ = bf16[15,2,96,128]{3,2,1,0:T(8,128)(2,1)} collective-permute-done((bf16[15,2,96,128]{3,2,1,0:T(8,128)(2,1)}, bf16[15,2,96,128]{3,2,1,0:T(8,128)(2,1)}, u32[]{:S(2)}, u32[]{:S(2)}) %collective-permute-start.25) | collective-permute-done | bytes 737312 | tf_op jit(solution)/shard_map/cond/branch_2_fun/ppermute | solution.py:455
  34.4 0.4 collective-permute-start.26
  34.8 0.1 collective-permute-start.27
  35.0 1.9 %collective-permute-done.26.refs_8_ = bf16[15,2,96,128]{3,2,1,0:T(8,128)(2,1)S(1)} collective-permute-done((bf16[15,2,96,128]{3,2,1,0:T(8,128)(2,1)}, bf16[15,2,96,128]{3,2,1,0:T(8,128)(2,1)S(1)}, u32[]{:S(2)}, u32[]{:S(2)}) %collective-permute-start.26) | collective-permute-done | bytes 737312 | tf_op jit(solution)/shard_map/cond/branch_2_fun/ppermute | solution.py:458
  36.9 0.0 copy-start.12
  36.9 3.7 %collective-permute-start.29 = (bf16[3,2,384,128]{3,2,1,0:T(8,128)(2,1)}, bf16[3,2,384,128]{3,2,1,0:T(8,128)(2,1)}, u32[]{:S(2)}, u32[]{:S(2)}) collective-permute-start(bf16[3,2,384,128]{3,2,1,0:T(8,128)(2,1)} %get-tuple-element.169.refs_1_), channel_id=1, source_target_pairs={{1,16},{17,32},{33,48},{49,64},{65,80},{81,96},{97,112},{16,1},{32... | collective-permute-start | bytes 1769480 | tf_op jit(solution)/shard_map/cond/branch_2_fun/ppermute | solution.py:474
  40.6 0.0 collective-permute-done.27.refs_9_
  40.6 0.0 copy-start.13
  40.6 0.1 collective-permute-start.28
  40.7 0.0 copy-start.6
  40.7 9.1 %branch_2_fun.8.refs_0_ = bf16[9,384,128]{2,1,0:T(8,128)(2,1)} custom-call(s32[8,20]{1,0:T(8,128)S(1)} %get-tuple-element.148.meta_ref, s32[8]{0:T(128)S(1)} %get-tuple-element.149.flag_ref, f32[2,96,96]{2,1,0:T(8,128)} %get-tuple-element.150.mask_ref, bf16[9,1,384,128]{3,2,1,0:T(8,128)(2,1)} %get-tuple-element.172.refs_0_, ...), custom_call_target="tpu_custom_call" | custom-call | tf_op jit(solution)/shard_map/cond/branch_2_fun/pallas_call | solution.py:422
  49.8 0.0 copy-done.12
  49.8 0.0 copy-done.13
  49.8 0.0 collective-permute-done.31.refs_3_
  49.9 1.2 %fusion.3 = (bf16[8,2,96,128]{3,2,1,0:T(8,128)(2,1)S(1)}, bf16[8,2,96,128]{3,2,1,0:T(8,128)(2,1)S(1)}) fusion(bf16[8,2,384,128]{3,2,1,0:T(8,128)(2,1)} %collective-permute-done.31.refs_3_), kind=kLoop, calls=%fused_computation.4 | loop fusion | bytes 1572864 | tf_op jit(solution)/shard_map/cond/branch_2_fun/slice | solution.py:463
  51.0 3.9 %collective-permute-start.32 = (bf16[8,2,96,128]{3,2,1,0:T(8,128)(2,1)S(1)}, bf16[8,2,96,128]{3,2,1,0:T(8,128)(2,1)S(1)}, u32[]{:S(2)}, u32[]{:S(2)}) collective-permute-start(bf16[8,2,96,128]{3,2,1,0:T(8,128)(2,1)S(1)} %get-tuple-element.240), channel_id=1, source_target_pairs={{0,2},{2,4},{4,6},{6,8},{8,10},{10,12},{12,14},{1,3},{3,5},{5,7},{... | collective-permute-start | bytes 1179656 | tf_op jit(solution)/shard_map/cond/branch_2_fun/ppermute | solution.py:462
  55.0 0.0 collective-permute-done.34.refs_2_.refs_6_
  55.0 21.2 %collective-permute-start.33 = (bf16[8,2,96,128]{3,2,1,0:T(8,128)(2,1)S(1)}, bf16[8,2,96,128]{3,2,1,0:T(8,128)(2,1)S(1)}, u32[]{:S(2)}, u32[]{:S(2)}) collective-permute-start(bf16[8,2,96,128]{3,2,1,0:T(8,128)(2,1)S(1)} %get-tuple-element.239), channel_id=1, source_target_pairs={{2,0},{4,2},{6,4},{8,6},{10,8},{12,10},{14,12},{3,1},{5,3},{7,5},{... | collective-permute-start | bytes 1179656 | tf_op jit(solution)/shard_map/cond/branch_2_fun/ppermute | solution.py:463
  76.2 0.0 copy-done.6
  76.2 10.9 %branch_2_fun.9.refs_7_ = f32[384,5120]{1,0:T(8,128)} custom-call(s32[8,20]{1,0:T(8,128)S(1)} %get-tuple-element.148.meta_ref, s32[8]{0:T(128)S(1)} %get-tuple-element.149.flag_ref, f32[2,96,96]{2,1,0:T(8,128)S(1)} %copy-done.6, bf16[9,384,128]{2,1,0:T(8,128)(2,1)} %branch_2_fun.8.refs_0_, bf16[1280,5120]{1,0:T(8,128)(2,1)} %get-tuple-element.178.refs_1_.refs_5_, ...), custom_call_target="tpu_custom_call" | custom-call | tf_op jit(solution)/shard_map/cond/branch_2_fun/pallas_call | solution.py:422
  87.2 0.0 collective-permute-done.32.refs_4_
  87.2 0.0 copy-start.20
  87.2 0.0 collective-permute-done.33.refs_5_
  87.2 0.0 copy-start.21
  87.2 0.0 collective-permute-done.30.refs_2_
  87.2 0.7 copy-done.20
  87.9 0.1 copy-done.21
  88.1 10.8 %branch_2_fun.10.refs_4_ = bf16[8,384,128]{2,1,0:T(8,128)(2,1)} custom-call(s32[8,20]{1,0:T(8,128)S(1)} %get-tuple-element.148.meta_ref, s32[8]{0:T(128)S(1)} %get-tuple-element.149.flag_ref, f32[2,96,96]{2,1,0:T(8,128)S(1)} %copy-done.6, bf16[8,1,384,128]{3,2,1,0:T(8,128)(2,1)} %get-tuple-element.170.refs_0_, ...), custom_call_target="tpu_custom_call" | custom-call | tf_op jit(solution)/shard_map/cond/branch_2_fun/pallas_call | solution.py:422
  98.9 0.0 collective-permute-done.29.refs_3_
  98.9 0.0 collective-permute-done.28.refs_2_
  98.9 14.6 %branch_2_fun.11 = bf16[384,5120]{1,0:T(8,128)(2,1)} custom-call(s32[8,20]{1,0:T(8,128)S(1)} %get-tuple-element.148.meta_ref, s32[8]{0:T(128)S(1)} %get-tuple-element.149.flag_ref, f32[2,96,96]{2,1,0:T(8,128)S(1)} %copy-done.6, bf16[3,1,384,128]{3,2,1,0:T(8,128)(2,1)} %get-tuple-element.168.refs_0_, bf16[3,2,384,128]{3,2,1,0:T(8,128)(2,1)} %get-tuple-element.169.refs_1_, ...), custom_call_target="tpu_custom_call" | custom-call | tf_op jit(solution)/shard_map/cond/branch_2_fun/pallas_call | solution.py:422
  (1 shorter events, 0.0 us)
Async XLA Ops:
  2.7 52.3 %collective-permute-start.34 = (bf16[1280,5120]{1,0:T(8,128)(2,1)}, bf16[1280,5120]{1,0:T(8,128)(2,1)}, u32[]{:S(2)}, u32[]{:S(2)}) collective-permute-start(bf16[1280,5120]{1,0:T(8,128)(2,1)} %get-tuple-element.178.refs_1_.refs_5_), channel_id=1, source_target_pairs={{0,1},{1,0},{2,3},{3,2},{4,5},{5,4},{6,7},{7,6},{8,9},{9,8},{10,11... | collective-permute-start | bytes 39321608 | tf_op jit(solution)/shard_map/cond/branch_2_fun/ppermute | solution.py:476
  3.4 13.7 %copy-start.2 = (bf16[384,2560]{1,0:T(8,128)(2,1)S(1)}, bf16[384,2560]{1,0:T(8,128)(2,1)}, u32[]{:S(2)}) copy-start(bf16[384,2560]{1,0:T(8,128)(2,1)} %get-tuple-element.153.refs_2_) | copy-start | bytes 5898244 | tf_op jit(solution)/shard_map/cond
  7.5 42.3 %collective-permute-start.31 = (bf16[8,2,384,128]{3,2,1,0:T(8,128)(2,1)}, bf16[8,2,384,128]{3,2,1,0:T(8,128)(2,1)}, u32[]{:S(2)}, u32[]{:S(2)}) collective-permute-start(bf16[8,2,384,128]{3,2,1,0:T(8,128)(2,1)} %get-tuple-element.171.refs_1_), channel_id=1, source_target_pairs={{1,16},{17,32},{33,48},{49,64},{65,80},{81,96},{97,112},{16,1},{32... | collective-permute-start | bytes 4718600 | tf_op jit(solution)/shard_map/cond/branch_2_fun/ppermute | solution.py:474
  10.8 20.3 %collective-permute-start.24 = (bf16[15,2,96,128]{3,2,1,0:T(8,128)(2,1)}, bf16[15,2,96,128]{3,2,1,0:T(8,128)(2,1)}, u32[]{:S(2)}, u32[]{:S(2)}) collective-permute-start(bf16[15,2,96,128]{3,2,1,0:T(8,128)(2,1)} %get-tuple-element.155), channel_id=1, source_target_pairs={{0,2},{2,4},{4,6},{6,8},{8,10},{10,12},{12,14},{1,3},{3,5},{5,7},{... | collective-permute-start | bytes 2211848 | tf_op jit(solution)/shard_map/cond/branch_2_fun/ppermute | solution.py:455
  14.0 20.5 %collective-permute-start.25 = (bf16[15,2,96,128]{3,2,1,0:T(8,128)(2,1)}, bf16[15,2,96,128]{3,2,1,0:T(8,128)(2,1)}, u32[]{:S(2)}, u32[]{:S(2)}) collective-permute-start(bf16[15,2,96,128]{3,2,1,0:T(8,128)(2,1)} %get-tuple-element.156), channel_id=1, source_target_pairs={{2,0},{4,2},{6,4},{8,6},{10,8},{12,10},{14,12},{3,1},{5,3},{7,5},{... | collective-permute-start | bytes 2211848 | tf_op jit(solution)/shard_map/cond/branch_2_fun/ppermute | solution.py:455
  17.0 70.2 %collective-permute-start.30 = (bf16[8,2,384,128]{3,2,1,0:T(8,128)(2,1)}, bf16[8,2,384,128]{3,2,1,0:T(8,128)(2,1)}, u32[]{:S(2)}, u32[]{:S(2)}) collective-permute-start(bf16[8,2,384,128]{3,2,1,0:T(8,128)(2,1)} %get-tuple-element.171.refs_1_), channel_id=1, source_target_pairs={{0,1},{1,0},{2,3},{3,2},{4,5},{5,4},{6,7},{7,6},{8,9},{9,8},{10,11... | collective-permute-start | bytes 4718600 | tf_op jit(solution)/shard_map/cond/branch_2_fun/ppermute | solution.py:475
  34.4 2.4 %collective-permute-start.26 = (bf16[15,2,96,128]{3,2,1,0:T(8,128)(2,1)}, bf16[15,2,96,128]{3,2,1,0:T(8,128)(2,1)S(1)}, u32[]{:S(2)}, u32[]{:S(2)}) collective-permute-start(bf16[15,2,96,128]{3,2,1,0:T(8,128)(2,1)} %collective-permute-done.24.refs_2_.refs_6_), channel_id=1, source_target_pairs={{0,1},{1,0},{2,3},{3,2},{4,5},{5,4},{6,7},{7,6},{8,9},{9,8},{10,11... | collective-permute-start | bytes 2211848 | tf_op jit(solution)/shard_map/cond/branch_2_fun/ppermute | solution.py:458
  34.8 5.8 %collective-permute-start.27 = (bf16[15,2,96,128]{3,2,1,0:T(8,128)(2,1)}, bf16[15,2,96,128]{3,2,1,0:T(8,128)(2,1)S(1)}, u32[]{:S(2)}, u32[]{:S(2)}) collective-permute-start(bf16[15,2,96,128]{3,2,1,0:T(8,128)(2,1)} %collective-permute-done.25.refs_3_.refs_7_), channel_id=1, source_target_pairs={{0,1},{1,0},{2,3},{3,2},{4,5},{5,4},{6,7},{7,6},{8,9},{9,8},{10,11... | collective-permute-start | bytes 2211848 | tf_op jit(solution)/shard_map/cond/branch_2_fun/ppermute | solution.py:458
  36.9 12.9 %copy-start.12 = (bf16[15,2,96,128]{3,2,1,0:T(8,128)(2,1)}, bf16[15,2,96,128]{3,2,1,0:T(8,128)(2,1)S(1)}, u32[]{:S(2)}) copy-start(bf16[15,2,96,128]{3,2,1,0:T(8,128)(2,1)S(1)} %collective-permute-done.26.refs_8_) | copy-start | bytes 2211844 | tf_op jit(solution)/shard_map/cond
  36.9 62.0 %collective-permute-start.29 = (bf16[3,2,384,128]{3,2,1,0:T(8,128)(2,1)}, bf16[3,2,384,128]{3,2,1,0:T(8,128)(2,1)}, u32[]{:S(2)}, u32[]{:S(2)}) collective-permute-start(bf16[3,2,384,128]{3,2,1,0:T(8,128)(2,1)} %get-tuple-element.169.refs_1_), channel_id=1, source_target_pairs={{1,16},{17,32},{33,48},{49,64},{65,80},{81,96},{97,112},{16,1},{32... | collective-permute-start | bytes 1769480 | tf_op jit(solution)/shard_map/cond/branch_2_fun/ppermute | solution.py:474
  40.6 9.2 %copy-start.13 = (bf16[15,2,96,128]{3,2,1,0:T(8,128)(2,1)}, bf16[15,2,96,128]{3,2,1,0:T(8,128)(2,1)S(1)}, u32[]{:S(2)}) copy-start(bf16[15,2,96,128]{3,2,1,0:T(8,128)(2,1)S(1)} %collective-permute-done.27.refs_9_) | copy-start | bytes 2211844 | tf_op jit(solution)/shard_map/cond
  40.6 58.2 %collective-permute-start.28 = (bf16[3,2,384,128]{3,2,1,0:T(8,128)(2,1)}, bf16[3,2,384,128]{3,2,1,0:T(8,128)(2,1)}, u32[]{:S(2)}, u32[]{:S(2)}) collective-permute-start(bf16[3,2,384,128]{3,2,1,0:T(8,128)(2,1)} %get-tuple-element.169.refs_1_), channel_id=1, source_target_pairs={{0,1},{1,0},{2,3},{3,2},{4,5},{5,4},{6,7},{7,6},{8,9},{9,8},{10,11... | collective-permute-start | bytes 1769480 | tf_op jit(solution)/shard_map/cond/branch_2_fun/ppermute | solution.py:475
  40.7 35.5 %copy-start.6 = (f32[2,96,96]{2,1,0:T(8,128)S(1)}, f32[2,96,96]{2,1,0:T(8,128)}, u32[]{:S(2)}) copy-start(f32[2,96,96]{2,1,0:T(8,128)} %get-tuple-element.150.mask_ref) | copy-start | bytes 221188 | tf_op jit(solution)/shard_map/cond
  51.0 36.1 %collective-permute-start.32 = (bf16[8,2,96,128]{3,2,1,0:T(8,128)(2,1)S(1)}, bf16[8,2,96,128]{3,2,1,0:T(8,128)(2,1)S(1)}, u32[]{:S(2)}, u32[]{:S(2)}) collective-permute-start(bf16[8,2,96,128]{3,2,1,0:T(8,128)(2,1)S(1)} %get-tuple-element.240), channel_id=1, source_target_pairs={{0,2},{2,4},{4,6},{6,8},{8,10},{10,12},{12,14},{1,3},{3,5},{5,7},{... | collective-permute-start | bytes 1179656 | tf_op jit(solution)/shard_map/cond/branch_2_fun/ppermute | solution.py:462
  55.0 32.2 %collective-permute-start.33 = (bf16[8,2,96,128]{3,2,1,0:T(8,128)(2,1)S(1)}, bf16[8,2,96,128]{3,2,1,0:T(8,128)(2,1)S(1)}, u32[]{:S(2)}, u32[]{:S(2)}) collective-permute-start(bf16[8,2,96,128]{3,2,1,0:T(8,128)(2,1)S(1)} %get-tuple-element.239), channel_id=1, source_target_pairs={{2,0},{4,2},{6,4},{8,6},{10,8},{12,10},{14,12},{3,1},{5,3},{7,5},{... | collective-permute-start | bytes 1179656 | tf_op jit(solution)/shard_map/cond/branch_2_fun/ppermute | solution.py:463
  87.2 0.7 copy-start.20
  87.2 0.9 copy-start.21
